TPU v7x, 512 devices: a whole 4x4x16 slice. The times are simulated.
512 devices in a mesh: dom: 512 (over x, y, z, core).
Axes of the slice: x: 4, y: 4, z: 16, core: 2. Of those that a mesh axis runs over, the one named last changes fastest.
Arguments:
- counts: float32 [64, 262144], P(None, 'dom'), may hold values from 0.5 to 8
- scaled_rate_constants: float32 [256], replicated, may hold values from 0.001 to 0.05
- reactant_species_index: int32 [2, 256], replicated, may hold values from 0 to 64
- product_species_index: int32 [2, 256], replicated, may hold values from 0 to 64
- leap_gaussian_noise: bfloat16 [256, 262144], P(None, 'dom'), may hold values from -5 to 5
- diff_rates: float32 [64], replicated, may hold values from 0.01 to 0.2
- face_weights: float32 [4, 262144], P(None, 'dom'), may hold values from 0.2 to 1.2
- face_target: int32 [4, 262144], P(None, 'dom'), may hold values from 0 to 1024, as said below
- recv_rows: int32 [2, 131072], P(None, 'dom'), may hold values from 0 to 512, as said below
- diff_noise: bfloat16 [4, 64, 262144], P(None, None, 'dom'), may hold values from -5 to 5
- tri_tet: int32 [262144], P('dom'), may hold values from 0 to 511
- tri_verts: int32 [3, 262144], P(None, 'dom'), may hold values from 0 to 767, as said below
- tri_area: float32 [262144], P('dom'), may hold values from 0.5 to 1.5
- voltage_old: float32 [131072], P('dom')
- mass: float32 [131072], P('dom'), may hold values from 0.5 to 4
- mat_cols: int32 [8, 131072], P(None, 'dom'), may hold values from 0 to 767, as said below
- mat_vals: float32 [8, 131072], P(None, 'dom'), may hold values from -1 to -0.2
Outputs:
- counts_new: float32 [64, 262144], P(None, 'dom')
- voltage_new: float32 [131072], P('dom')
Inputs may be any that keep to these rules, and one draw needn't show every extreme that they name: `face_target`: each entry is a tetrahedron of the same partition (below 512), send slot k = entry - 512 (slots below 256 lead to the partition before, the others to the partition after), or 1024 for a wall. Each send slot is named by at most one face. Send slot 256 + i of a partition and slot i of the partition after describe the same pair of tetrahedra, in opposite directions; the used slots towards a neighbour are the lowest ones; the first partition sends nothing before it and the last nothing after it. Some pair of neighbouring partitions is joined by exactly 256 faces. `recv_rows`: entry i of row 0 of a partition is the tetrahedron joined to send slot 256 + i of the partition before, entry i of row 1 the one joined to send slot i of the partition after, or 512 where that slot is unused; the entries of one row of one partition that are below 512 are distinct. `tri_verts`: the first partition names no vertex before it, the last none after it. `mat_cols`: encoded as tri_verts. Slots 0, 1, 4, 5 name vertices of the own partition, slots 2, 3 of the partition after, slots 6, 7 of the partition before; with mat_vals the off-diagonal entries between existing vertices are symmetric.
All inputs are finite; a program needn't handle non-finite values.
Results may differ from a plain program's by a relative error of at most 0.0003.
Values sent between devices are 32-bit elements; how exact they have to be, the bound alone decides.
A program may use at most 64 MiB of HBM per device.

v0:
```python
import math

import jax
import jax.numpy as jnp
from jax import lax
from jax.sharding import PartitionSpec as P

ITERS = 2


BIG_LIMIT = 1e30
CURRENT_GAIN = 4.0
HALF_SATURATION = 2.0


def extended_2(shard, sides, width):
    for axis, dim in sides:
        size, length = (lax.axis_size(axis), shard.shape[dim])
        up = [(i, (i + 1) % size) for i in range(size - 1)]
        down = [(j, i) for i, j in up]
        last = lax.slice_in_dim(shard, length - width, length, axis=dim)
        initial = lax.slice_in_dim(shard, 0, width, axis=dim)
        before = lax.ppermute(last, axis, up)
        after = lax.ppermute(initial, axis, down)
        shard = jnp.concatenate([before, shard, after], axis=dim)
    return shard


def tau_leap_events(partial_counts, scaled_rate_constants, reactant_species_index, partial_noise):
    species = partial_counts.shape[0]
    extended = jnp.concatenate(
        [partial_counts, jnp.ones((1, partial_counts.shape[1]), jnp.float32)], axis=0
    )
    first_in = jnp.take(extended, reactant_species_index[0], axis=0)
    second_in = jnp.take(extended, reactant_species_index[1], axis=0)
    propensity = scaled_rate_constants[:, None] * first_in * second_in
    limit_first = jnp.where((reactant_species_index[0] < species)[:, None], first_in, BIG_LIMIT)
    limit_second = jnp.where((reactant_species_index[1] < species)[:, None], second_in, BIG_LIMIT)
    limit_all = jnp.minimum(limit_first, limit_second)
    raw_leap = propensity + jnp.sqrt(propensity) * partial_noise.astype(jnp.float32)
    return jnp.minimum(jnp.maximum(raw_leap, 0.0), limit_all)


def diffusion_amounts(reacted, diff_rates, weights, targets, partial_noise, wall_slot):
    hop_prob = diff_rates[None, :, None] * weights[:, None, :]
    mean_hop = reacted[None, :, :] * hop_prob
    spread_hop = jnp.sqrt(mean_hop * (1.0 - hop_prob))
    raw_hop = jnp.maximum(mean_hop + spread_hop * partial_noise.astype(jnp.float32), 0.0)
    raw_hop = jnp.where((targets == wall_slot)[:, None, :], 0.0, raw_hop)
    total_out = jnp.sum(raw_hop, axis=0)
    factor = jnp.minimum(1.0, reacted / jnp.maximum(total_out, 1.0))
    return raw_hop * factor[None, :, :]


def deposit_faces(amount, targets, width):
    faces, species, tet_count = amount.shape
    block = math.gcd(tet_count, 256)
    blocks = tet_count // block
    amount_blocks = (
        amount.reshape(faces, species, blocks, block)
        .transpose(2, 1, 0, 3)
        .reshape(blocks, species, faces * block)
    )
    target_blocks = (
        targets.reshape(faces, blocks, block).transpose(1, 0, 2).reshape(blocks, faces * block)
    )
    columns = lax.broadcasted_iota(jnp.int32, (1, width), 1)

    def add_block(total, pieces):
        amount_piece, target_piece = pieces
        onehot = (target_piece[:, None] == columns).astype(jnp.float32)
        return (
            total
            + jnp.dot(
                amount_piece,
                onehot,
                precision=lax.Precision.HIGHEST,
                preferred_element_type=jnp.float32,
            ),
            None,
        )

    total, unused = lax.scan(
        add_block, jnp.zeros((species, width), jnp.float32), (amount_blocks, target_blocks)
    )
    return total


def per_device(
    counts,
    scaled_rate_constants,
    reactant_species_index,
    product_species_index,
    leap_gaussian_noise,
    diff_rates,
    face_weights,
    face_target,
    recv_rows,
    diff_noise,
    tri_tet,
    tri_verts,
    tri_area,
    voltage_old,
    mass,
    mat_cols,
    mat_vals,
):
    species, tet_count = counts.shape
    bnd_count = recv_rows.shape[1]
    vertex_count = voltage_old.shape[0]
    wall_slot = tet_count + 2 * bnd_count
    reaction_events = tau_leap_events(
        counts, scaled_rate_constants, reactant_species_index, leap_gaussian_noise
    )
    levels = lax.broadcasted_iota(jnp.int32, (species, scaled_rate_constants.shape[0]), 0)

    def indicator(species_ids):
        return (levels == species_ids[None, :]).astype(jnp.float32)

    stoichiometry = (
        indicator(product_species_index[0])
        + indicator(product_species_index[1])
        - indicator(reactant_species_index[0])
        - indicator(reactant_species_index[1])
    )
    count_delta = jnp.dot(
        stoichiometry,
        reaction_events,
        precision=lax.Precision.HIGHEST,
        preferred_element_type=jnp.float32,
    )
    reacted = jnp.maximum(counts + count_delta, 0.0)
    amount = diffusion_amounts(
        reacted, diff_rates, face_weights, face_target, diff_noise, wall_slot
    )
    remaining = reacted - jnp.sum(amount, axis=0)
    deposited = deposit_faces(amount, face_target, wall_slot)
    inflow = deposited[:, :tet_count]
    outgoing = deposited[:, tet_count:wall_slot]
    arrived = extended_2(outgoing, (("dom", 1),), bnd_count)
    both_sides = jnp.concatenate([arrived[:, :bnd_count], arrived[:, 3 * bnd_count :]], axis=1)
    recv_all = jnp.concatenate([recv_rows[0], recv_rows[1]])
    tet_columns = lax.broadcasted_iota(jnp.int32, (1, tet_count), 1)
    recv_onehot = (recv_all[:, None] == tet_columns).astype(jnp.float32)
    received = jnp.dot(
        both_sides, recv_onehot, precision=lax.Precision.HIGHEST, preferred_element_type=jnp.float32
    )
    counts_new = remaining + inflow + received
    calcium = jnp.take(counts_new[0], tri_tet)
    share_each = CURRENT_GAIN * tri_area * calcium / (calcium + HALF_SATURATION) / 3.0
    vertex_columns = lax.broadcasted_iota(jnp.int32, (1, 3 * vertex_count), 1)
    corner_onehot = (tri_verts[0][:, None] == vertex_columns).astype(jnp.float32)
    corner_onehot = corner_onehot + (tri_verts[1][:, None] == vertex_columns).astype(jnp.float32)
    corner_onehot = corner_onehot + (tri_verts[2][:, None] == vertex_columns).astype(jnp.float32)
    deposit = jnp.dot(
        share_each[None, :],
        corner_onehot,
        precision=lax.Precision.HIGHEST,
        preferred_element_type=jnp.float32,
    )[0]
    side_blocks = jnp.concatenate([deposit[:vertex_count], deposit[2 * vertex_count :]])
    current_rows = extended_2(side_blocks, (("dom", 0),), vertex_count)
    start_extended = extended_2(voltage_old, (("dom", 0),), vertex_count)
    injected = (
        deposit[vertex_count : 2 * vertex_count]
        + current_rows[:vertex_count]
        + current_rows[3 * vertex_count :]
    )
    rhs = mass * voltage_old + injected
    diagonal = mass + jnp.sum(jnp.abs(mat_vals), axis=0)

    def apply_matrix(extended, field):
        return diagonal * field + jnp.sum(mat_vals * jnp.take(extended, mat_cols), axis=0)

    def squares_sum(field):
        return lax.psum(jnp.sum(field * field), "dom")

    solution = voltage_old
    residual = rhs - apply_matrix(start_extended, voltage_old)
    direction = residual
    norm_now = squares_sum(residual)
    for turn_index in range(ITERS):
        image = apply_matrix(extended_2(direction, (("dom", 0),), vertex_count), direction)
        alpha = norm_now / lax.psum(jnp.sum(direction * image), "dom")
        solution = solution + alpha * direction
        residual = residual - alpha * image
        norm_next = squares_sum(residual)
        direction = residual + norm_next / norm_now * direction
        norm_now = norm_next
    return (counts_new, solution)


def solution(mesh):
    placed = (
        P(None, "dom"),
        P(),
        P(),
        P(),
        P(None, "dom"),
        P(),
        P(None, "dom"),
        P(None, "dom"),
        P(None, "dom"),
        P(None, None, "dom"),
        P("dom"),
        P(None, "dom"),
        P("dom"),
        P("dom"),
        P("dom"),
        P(None, "dom"),
        P(None, "dom"),
    )
    return jax.shard_map(
        per_device,
        mesh=mesh,
        in_specs=placed,
        out_specs=(P(None, "dom"), P("dom")),
        check_vma=False,
    )
```

profile of v0, /device:TPU:1, one launch (start us, length us, event | category | flops | bytes accessed | tf_op | source)
XLA Modules:
  0.0 413.0 jit_solution(2152257537506085400)
XLA Ops:
  0.6 4.9 %collective-permute-start.4 = (f32[256]{0:T(256)}, f32[256]{0:T(256)S(1)}, u32[]{:S(2)}, u32[]{:S(2)}) collective-permute-start(f32[256]{0:T(256)} %param.36), channel_id=1, source_target_pairs={{0,1},{1,2},{2,3},{3,4},{4,5},{5,6},{6,7},{7,8},{8,9},{9,10},{10,1... | collective-permute-start | bytes 3080 | tf_op jit(solution)/shard_map/ppermute | solution.py:23
  5.6 5.1 %collective-permute-start.5 = (f32[256]{0:T(256)}, f32[256]{0:T(256)S(1)}, u32[]{:S(2)}, u32[]{:S(2)}) collective-permute-start(f32[256]{0:T(256)} %param.36), channel_id=1, source_target_pairs={{1,0},{2,1},{3,2},{4,3},{5,4},{6,5},{7,6},{8,7},{9,8},{10,9},{11,1... | collective-permute-start | bytes 3080 | tf_op jit(solution)/shard_map/ppermute | solution.py:24
  10.7 0.8 fusion.80
  11.6 0.9 concatenate.18
  12.5 1.0 gather_fusion.1
  13.4 0.0 copy-start.11
  13.5 0.0 copy-start.15
  13.5 0.0 copy-start.16
  13.5 1.0 gather_fusion.2
  14.6 0.0 copy-start
  14.6 0.9 fusion.14
  15.5 0.0 copy-done
  15.5 0.4 fusion.42
  15.9 0.4 fusion.74
  16.3 0.3 reshape.58
  16.6 0.3 copy.26
  17.0 0.3 reshape.59
  17.3 0.0 copy-start.12
  17.3 0.0 copy-start.8
  17.3 0.0 copy-start.7
  17.4 3.7 while.11
  17.4 1.8 fusion.86
  19.2 1.8 fusion.86
  21.0 1.9 collective-permute-start
  23.0 2.4 collective-permute-start.1
  25.6 8.6 %gather_fusion.3 = f32[2048]{0:T(1024)S(1)} fusion(f32[768]{0:T(1024)S(1)} %pad_maximum_fusion, s32[2048]{0:T(1024)S(1)} %broadcast_clamp_fusion), kind=kCustom, calls=%fused_computation.1.clone | custom fusion | bytes 24576 | tf_op jit(solution)/shard_map/jit(_take)/gather | solution.py:173
  34.2 0.6 convolution_add_fusion
  34.8 3.5 gather_fusion
  38.3 0.0 copy-start.14
  38.4 1.4 fusion.15
  39.8 3.2 collective-permute-start.2
  43.0 1.9 collective-permute-start.3
  45.0 2.9 collective-permute-done.3
  47.9 2.0 collective-permute-start.6
  49.9 2.4 collective-permute-start.7
  52.2 2.5 collective-permute-done.7
  54.7 8.6 %gather_fusion.4 = f32[2048]{0:T(1024)S(1)} fusion(f32[768]{0:T(1024)S(1)} %pad_maximum_fusion.1, s32[2048]{0:T(1024)S(1)} %broadcast_clamp_fusion), kind=kCustom, calls=%fused_computation.3.clone | custom fusion | bytes 24576 | tf_op jit(solution)/shard_map/jit(_take)/gather | solution.py:173
  63.4 0.7 multiply_reduce_fusion.2
  64.1 122.2 %all-reduce.1 = (f32[]{:T(128)}, f32[]{:T(128)}) all-reduce(f32[]{:T(128)} %get-tuple-element.52, f32[]{:T(128)} %get-tuple-element.51), channel_id=1, replica_groups=mesh['dom'=512] {'dom'}, use_global_device_ids=true, to_apply=%region_7.10 | all-reduce | flops 2 | bytes 16 | tf_op jit(solution)/shard_map/psum | solution.py:176
  187.5 0.6 multiply_reduce_fusion.1
  188.1 99.2 %psum.30 = f32[]{:T(128)} all-reduce(f32[]{:T(128)} %multiply_reduce_fusion.1), channel_id=1, replica_groups=mesh['dom'=512] {'dom'}, use_global_device_ids=true, to_apply=%region_12.15 | all-reduce | flops 1 | bytes 8 | tf_op jit(solution)/shard_map/psum | solution.py:176
  288.6 4.2 %collective-permute-start.8 = (f32[256]{0:T(256)S(1)}, f32[256]{0:T(256)S(1)}, u32[]{:S(2)}, u32[]{:S(2)}) collective-permute-start(f32[256]{0:T(256)S(1)} %multiply_add_fusion.1), channel_id=1, source_target_pairs={{0,1},{1,2},{2,3},{3,4},{4,5},{5,6},{6,7},{7,8},{8,9},{9,10},{10,1... | collective-permute-start | bytes 3080 | tf_op jit(solution)/shard_map/ppermute | solution.py:23
  292.8 1.9 collective-permute-start.9
  294.7 2.9 collective-permute-done.9
  297.7 8.6 %gather_fusion.5 = f32[2048]{0:T(1024)S(1)} fusion(f32[768]{0:T(1024)S(1)} %pad_maximum_fusion.2, s32[2048]{0:T(1024)S(1)} %broadcast_clamp_fusion), kind=kCustom, calls=%fused_computation.4.clone | custom fusion | bytes 24576 | tf_op jit(solution)/shard_map/jit(_take)/gather | solution.py:173
  306.3 0.7 multiply_reduce_fusion
  307.0 104.0 %psum.31 = f32[]{:T(128)} all-reduce(f32[]{:T(128)} %multiply_reduce_fusion), channel_id=1, replica_groups=mesh['dom'=512] {'dom'}, use_global_device_ids=true, to_apply=%region_15.18 | all-reduce | flops 1 | bytes 8 | tf_op jit(solution)/shard_map/psum | solution.py:184
  412.4 0.6 multiply_add_fusion
  (67 shorter events, 0.4 us)
Async XLA Ops:
  0.6 24.9 %collective-permute-start.4 = (f32[256]{0:T(256)}, f32[256]{0:T(256)S(1)}, u32[]{:S(2)}, u32[]{:S(2)}) collective-permute-start(f32[256]{0:T(256)} %param.36), channel_id=1, source_target_pairs={{0,1},{1,2},{2,3},{3,4},{4,5},{5,6},{6,7},{7,8},{8,9},{9,10},{10,1... | collective-permute-start | bytes 3080 | tf_op jit(solution)/shard_map/ppermute | solution.py:23
  5.6 20.0 %collective-permute-start.5 = (f32[256]{0:T(256)}, f32[256]{0:T(256)S(1)}, u32[]{:S(2)}, u32[]{:S(2)}) collective-permute-start(f32[256]{0:T(256)} %param.36), channel_id=1, source_target_pairs={{1,0},{2,1},{3,2},{4,3},{5,4},{6,5},{7,6},{8,7},{9,8},{10,9},{11,1... | collective-permute-start | bytes 3080 | tf_op jit(solution)/shard_map/ppermute | solution.py:24
  13.4 1.0 copy-start.11
  13.5 1.0 copy-start.6
  13.5 1.1 copy-start.2
  13.5 1.1 copy-start.15
  13.5 1.1 copy-start.16
  14.6 1.0 copy-start
  14.6 0.9 copy-start.4
  14.6 0.9 copy-start.10
  17.3 8.1 %copy-start.12 = (s32[2,256]{1,0:T(2,128)S(1)}, s32[2,256]{1,0:T(2,128)}, u32[]{:S(2)}) copy-start(s32[2,256]{1,0:T(2,128)} %param.31) | copy-start | bytes 6148
  17.3 8.1 %copy-start.8 = (s32[512]{0:T(512)S(1)}, s32[512]{0:T(512)}, u32[]{:S(2)}) copy-start(s32[512]{0:T(512)} %param.33) | copy-start | bytes 6148
  17.3 8.1 %copy-start.9 = (s32[3,512]{1,0:T(4,128)S(1)}, s32[3,512]{1,0:T(4,128)}, u32[]{:S(2)}) copy-start(s32[3,512]{1,0:T(4,128)} %param.34) | copy-start | bytes 18436
  17.3 8.1 %copy-start.5 = (s32[8,256]{1,0:T(8,128)S(1)}, s32[8,256]{1,0:T(8,128)}, u32[]{:S(2)}) copy-start(s32[8,256]{1,0:T(8,128)} %param.38) | copy-start | bytes 24580
  17.3 8.2 %copy-start.7 = (f32[256]{0:T(256)S(1)}, f32[256]{0:T(256)}, u32[]{:S(2)}) copy-start(f32[256]{0:T(256)} %param.36) | copy-start | bytes 3076
  21.0 13.1 %collective-permute-start = (f32[64,256]{1,0:T(8,128)S(1)}, f32[64,256]{1,0:T(8,128)S(1)}, u32[]{:S(2)}, u32[]{:S(2)}) collective-permute-start(f32[64,256]{1,0:T(8,128)S(1)} %get-tuple-element.68), channel_id=1, source_target_pairs={{0,1},{1,2},{2,3},{3,4},{4,5},{5,6},{6,7},{7,8},{8,9},{9,10},{10,1... | collective-permute-start | bytes 196616 | tf_op jit(solution)/shard_map/ppermute | solution.py:23
  23.0 11.2 %collective-permute-start.1 = (f32[64,256]{1,0:T(8,128)S(1)}, f32[64,256]{1,0:T(8,128)S(1)}, u32[]{:S(2)}, u32[]{:S(2)}) collective-permute-start(f32[64,256]{1,0:T(8,128)S(1)} %get-tuple-element.69), channel_id=1, source_target_pairs={{1,0},{2,1},{3,2},{4,3},{5,4},{6,5},{7,6},{8,7},{9,8},{10,9},{11,1... | collective-permute-start | bytes 196616 | tf_op jit(solution)/shard_map/ppermute | solution.py:24
  34.8 3.5 copy-start.1
  34.8 3.5 copy-start.13
  38.3 6.6 %copy-start.3 = (f32[8,256]{1,0:T(8,128)S(1)}, f32[8,256]{1,0:T(8,128)}, u32[]{:S(2)}) copy-start(f32[8,256]{1,0:T(8,128)} %param.39) | copy-start | bytes 24580
  38.3 9.5 %copy-start.14 = (f32[256]{0:T(256)S(1)}, f32[256]{0:T(256)}, u32[]{:S(2)}) copy-start(f32[256]{0:T(256)} %param.37) | copy-start | bytes 3076
  39.8 5.1 %collective-permute-start.2 = (f32[256]{0:T(256)S(1)}, f32[256]{0:T(256)S(1)}, u32[]{:S(2)}, u32[]{:S(2)}) collective-permute-start(f32[256]{0:T(256)S(1)} %get-tuple-element.73), channel_id=1, source_target_pairs={{0,1},{1,2},{2,3},{3,4},{4,5},{5,6},{6,7},{7,8},{8,9},{9,10},{10,1... | collective-permute-start | bytes 3080 | tf_op jit(solution)/shard_map/ppermute | solution.py:23
  43.0 4.9 %collective-permute-start.3 = (f32[256]{0:T(256)S(1)}, f32[256]{0:T(256)S(1)}, u32[]{:S(2)}, u32[]{:S(2)}) collective-permute-start(f32[256]{0:T(256)S(1)} %get-tuple-element.74), channel_id=1, source_target_pairs={{1,0},{2,1},{3,2},{4,3},{5,4},{6,5},{7,6},{8,7},{9,8},{10,9},{11,1... | collective-permute-start | bytes 3080 | tf_op jit(solution)/shard_map/ppermute | solution.py:24
  47.9 4.3 %collective-permute-start.6 = (f32[256]{0:T(256)S(1)}, f32[256]{0:T(256)S(1)}, u32[]{:S(2)}, u32[]{:S(2)}) collective-permute-start(f32[256]{0:T(256)S(1)} %get-tuple-element.63), channel_id=1, source_target_pairs={{0,1},{1,2},{2,3},{3,4},{4,5},{5,6},{6,7},{7,8},{8,9},{9,10},{10,1... | collective-permute-start | bytes 3080 | tf_op jit(solution)/shard_map/ppermute | solution.py:23
  49.9 4.9 %collective-permute-start.7 = (f32[256]{0:T(256)S(1)}, f32[256]{0:T(256)S(1)}, u32[]{:S(2)}, u32[]{:S(2)}) collective-permute-start(f32[256]{0:T(256)S(1)} %get-tuple-element.63), channel_id=1, source_target_pairs={{1,0},{2,1},{3,2},{4,3},{5,4},{6,5},{7,6},{8,7},{9,8},{10,9},{11,1... | collective-permute-start | bytes 3080 | tf_op jit(solution)/shard_map/ppermute | solution.py:24
  288.6 6.2 %collective-permute-start.8 = (f32[256]{0:T(256)S(1)}, f32[256]{0:T(256)S(1)}, u32[]{:S(2)}, u32[]{:S(2)}) collective-permute-start(f32[256]{0:T(256)S(1)} %multiply_add_fusion.1), channel_id=1, source_target_pairs={{0,1},{1,2},{2,3},{3,4},{4,5},{5,6},{6,7},{7,8},{8,9},{9,10},{10,1... | collective-permute-start | bytes 3080 | tf_op jit(solution)/shard_map/ppermute | solution.py:23
  292.8 4.9 %collective-permute-start.9 = (f32[256]{0:T(256)S(1)}, f32[256]{0:T(256)S(1)}, u32[]{:S(2)}, u32[]{:S(2)}) collective-permute-start(f32[256]{0:T(256)S(1)} %multiply_add_fusion.1), channel_id=1, source_target_pairs={{1,0},{2,1},{3,2},{4,3},{5,4},{6,5},{7,6},{8,7},{9,8},{10,9},{11,1... | collective-permute-start | bytes 3080 | tf_op jit(solution)/shard_map/ppermute | solution.py:24
where the time goes:
time: 414 us; the launch traced here: 413 us
  blocking collectives  325 us (79%)
  local copies, waits for them, and re-layouts  34 us (8%)
  starting transfers between devices  30 us (7%)
  waiting for transfers between devices  8.39 us (2%)
  matrix products  6.46 us (2%)
  between operations  5.17 us (1%)
    psum x2, blocking collectives, squares_sum(): return lax.psum(jnp.sum(field * field), 'dom')  221 us
    psum x1, blocking collectives, per_device(): alpha = norm_now / lax.psum(jnp.sum(direction * image), 'dom')  104 us
    gather x6, local copies, waits for them, and re-layouts, apply_matrix(): jnp.take(extended, mat_cols)  25.8 us
    ppermute x5, starting transfers between devices, extended_2(): before = lax.ppermute(last, axis, up)  16.2 us
    ppermute x5, starting transfers between devices, extended_2(): after = lax.ppermute(initial, axis, down)  13.8 us
    ppermute x5, waiting for transfers between devices, extended_2(): after = lax.ppermute(initial, axis, down)  8.37 us
  transfers between devices with their start and end apart: 10, of which 3 were waited for; matrix products, arithmetic and copies ran while one was open for 4% of the time, Pallas kernels for 0%

commit v1 on v0

v1 whole, which is shorter than its diff:
```python
import jax
import jax.numpy as jnp
from jax import lax
from jax.experimental import pallas as pl
from jax.experimental.pallas import tpu as pltpu
from jax.sharding import PartitionSpec as P

F32 = jnp.float32
BF16 = jnp.bfloat16
I32 = jnp.int32
MESH = pl.DeviceIdType.MESH

N = 512
S = 64
R = 256
T = 512
B = 256
V = 256
BIG = 1e30
SCALE = 1.0 / 32.0
ZG = 32
XY = 16


def nn(a, b):
    return lax.dot_general(a, b, (((1,), (0,)), ((), ())), preferred_element_type=F32)


def nt(a, b):
    return lax.dot_general(a, b, (((1,), (1,)), ((), ())), preferred_element_type=F32)


def iota(shape, dim):
    return lax.broadcasted_iota(I32, shape, dim)


def cut2(x):
    hi = x.astype(BF16)
    return hi, (x - hi.astype(F32)).astype(BF16)


def cut3(x):
    hi = x.astype(BF16)
    rest = x - hi.astype(F32)
    mid = rest.astype(BF16)
    return hi, mid, (rest - mid.astype(F32)).astype(BF16)


def rows3(x):
    hi = x.astype(BF16).astype(F32)
    rest = x - hi
    mid = rest.astype(BF16).astype(F32)
    low = rest - mid
    at = iota((16, x.shape[1]), 0)
    return jnp.where(at == 0, hi, jnp.where(at == 1, mid, jnp.where(at == 2, low, 0.0))).astype(BF16)


def add_rows(x):
    return jnp.sum(x, axis=0, keepdims=True)


def column(row, size):
    return jnp.sum(
        jnp.where(iota((size, size), 0) == iota((size, size), 1), row, 0.0), axis=1, keepdims=True
    )


def hot(cond):
    return jnp.where(cond, 1.0, 0.0).astype(BF16)


def build_matrix(cols, vals, mass, keep_before, keep_after, hi_ref, lo_ref):
    diag = (mass[...] + jnp.sum(jnp.abs(vals[...]), axis=0, keepdims=True)) * SCALE
    step = 64
    for block, slots in ((0, (6, 7)), (1, (0, 1, 4, 5)), (2, (2, 3))):
        for j0 in range(0, V, step):
            at = iota((step, V), 0) + (block * V + j0)
            total = jnp.zeros((step, V), F32)
            for k in slots:
                total = total + jnp.where(cols[k : k + 1, :] == at, vals[k : k + 1, :] * SCALE, 0.0)
            if block == 0:
                total = total * keep_before
            elif block == 2:
                total = total * keep_after
            else:
                total = total + jnp.where(iota((step, V), 1) == at - V, diag, 0.0)
            hi, lo = cut2(total)
            hi_ref[block * V + j0 : block * V + j0 + step, :] = hi
            lo_ref[block * V + j0 : block * V + j0 + step, :] = lo


def kernel(
    counts_h, rate_h, ri_h, pi_h, leap_h, dr_h, fw_h, ft_h, rr_h, dn_h, tt_h, tv_h, ta_h, v_h, m_h, mc_h, mv_h,
    out_h, vout_h,
    counts, rate, ri, pi, leap, dr, fw, ft, rrow, dn, tt, tv, ta, v, m, mc, mv,
    xs, fire, am, ot, loc, rt, gt, ct, bh, bl, nh, nl, arr, cnew, vnew,
    slots, slots_in, pk1, rx1, nc, nv, nm, pk2, rx2, red, red_a, red_b,
    in_sem, out_sem, send_sem, recv_sem,
):
    me = lax.axis_index("dom")
    hbm = (counts_h, rate_h, ri_h, pi_h, leap_h, dr_h, fw_h, ft_h, rr_h, dn_h, tt_h, tv_h, ta_h, v_h, m_h, mc_h, mv_h)
    vmem = (counts, rate, ri, pi, leap, dr, fw, ft, rrow, dn, tt, tv, ta, v, m, mc, mv)
    loads = [pltpu.make_async_copy(h, d, in_sem.at[i]) for i, (h, d) in enumerate(zip(hbm, vmem))]
    for i in (7, 2, 3, 1, 0, 4, 5, 6, 9, 8, 10, 11, 12, 13, 14, 15, 16):
        loads[i].start()

    def chain(offset):
        return lax.rem(me + (offset + N), N)

    z_base = (me // ZG) * ZG
    z_at = lax.rem(me, ZG)
    xy_at = me // ZG

    def z_partner(j):
        return z_base + lax.rem(z_at + j, ZG)

    def xy_partner(j):
        return lax.rem(xy_at + j, XY) * ZG + z_at

    barrier = pltpu.get_barrier_semaphore()
    greet = [chain(o) for o in (1, -1, 2, -2, 3, -3)]
    greet += [z_partner(j) for j in range(1, ZG)] + [xy_partner(j) for j in range(1, XY)]
    for other in greet:
        pl.semaphore_signal(barrier, inc=1, device_id=(other,), device_id_type=MESH)

    loads[7].wait()

    def build_targets(c, carry):
        at = iota((64, T), 0) + c * 64
        start = pl.multiple_of(c * 64, 64)
        for f in range(4):
            ot[pl.ds(start, 64), f * T : (f + 1) * T] = hot(ft[f : f + 1, :] == at)
        return carry

    lax.fori_loop(0, (T + 2 * B) // 64, build_targets, 0)

    for i in (0, 1, 2, 3, 4):
        loads[i].wait()
    for i, part in enumerate(cut3(counts[...])):
        xs[i * S : (i + 1) * S, :] = part
    xs[3 * S :, :] = jnp.ones((S, T), BF16)
    lane = iota((1, 256), 1)
    wanted = jnp.where(lane < 3 * S, lax.rem(lane, S), jnp.where(lane == 3 * S, S, -1)).astype(F32)
    first = column(ri[0:1, :].astype(F32), R)
    second = column(ri[1:2, :].astype(F32), R)
    rates = column(rate[...], R)
    cap_first = jnp.where(first == S, BIG, 0.0)
    cap_second = jnp.where(second == S, BIG, 0.0)
    step = 64
    for c in range(0, R, step):
        one = first[c : c + step, :]
        two = second[c : c + step, :]
        x1 = nn(hot(one == wanted), xs[...])
        x2 = nn(hot(two == wanted), xs[...])
        prop = rates[c : c + step, :] * x1 * x2
        limit = jnp.minimum(
            jnp.maximum(x1, cap_first[c : c + step, :]), jnp.maximum(x2, cap_second[c : c + step, :])
        )
        raw = prop + jnp.sqrt(prop) * leap[c : c + step, :].astype(F32)
        hi, lo = cut2(jnp.minimum(jnp.maximum(raw, 0.0), limit))
        fire[c : c + step, :] = hi
        fire[R + c : R + c + step, :] = lo
    level = iota((S, R), 0)

    def has(row):
        return jnp.where(row == level, 1.0, 0.0)

    stoich = (has(pi[0:1, :]) + has(pi[1:2, :]) - has(ri[0:1, :]) - has(ri[1:2, :])).astype(BF16)
    delta = nn(stoich, fire[0:R, :]) + nn(stoich, fire[R:, :])
    cnew[...] = jnp.maximum(counts[...] + delta, 0.0)

    for i in (5, 6, 9):
        loads[i].wait()
    hop = column(dr[...], S)
    step = 16
    for c in range(0, S, step):
        here = cnew[c : c + step, :]
        raws = []
        for f in range(4):
            prob = hop[c : c + step, :] * fw[f : f + 1, :]
            mean = here * prob
            spread = jnp.sqrt(mean * (1.0 - prob))
            raw = jnp.maximum(mean + spread * dn[f, c : c + step, :].astype(F32), 0.0)
            raws.append(jnp.where(ft[f : f + 1, :] == T + 2 * B, 0.0, raw))
        total = raws[0] + raws[1] + raws[2] + raws[3]
        factor = jnp.minimum(1.0, here / jnp.maximum(total, 1.0))
        for f in range(4):
            hi, lo = cut2(raws[f] * factor)
            am[c : c + step, f * T : (f + 1) * T] = hi
            am[S + c : S + c + step, f * T : (f + 1) * T] = lo
        loc[c : c + step, :] = here - total * factor
    for side in range(2):
        out = nt(am[...], ot[T + side * B : T + (side + 1) * B, :])
        slots[side] = out[:S, :] + out[S:, :]
    loads[13].wait()
    for side in range(2):
        pk1[side, :, 0:B] = slots[side, 0:1, :]
        pk1[side, :, B:] = v[...]

    for i in (14, 15, 16):
        loads[i].wait()
    pl.semaphore_wait(barrier, len(greet))
    sends = []

    def send(src, dst, sem, other):
        copy = pltpu.make_async_remote_copy(
            src_ref=src, dst_ref=dst, send_sem=send_sem.at[sem], recv_sem=recv_sem.at[sem],
            device_id=(other,), device_id_type=MESH,
        )
        copy.start()
        sends.append(copy)
        return copy

    before, after = chain(-1), chain(1)
    small = [send(pk1.at[1], rx1.at[0], 0, after), send(pk1.at[0], rx1.at[1], 1, before)]
    params = [send(mc, nc, 2, before), send(mv, nv, 3, before), send(m, nm, 4, before)]
    bulk = [send(slots.at[1], slots_in.at[0], 5, after), send(slots.at[0], slots_in.at[1], 6, before)]

    for w in range(0, T, 256):
        out = nt(am[...], ot[w : w + 256, :])
        loc[:, w : w + 256] = loc[:, w : w + 256] + out[:S, :] + out[S:, :]
    loads[8].wait()
    loads[10].wait()
    loads[11].wait()
    loads[12].wait()
    for c in range(0, T, 64):
        at = iota((64, B), 0) + c
        rt[c : c + 64, 0:B] = hot(rrow[0:1, :] == at)
        rt[c : c + 64, B:] = hot(rrow[1:2, :] == at)
        gt[c : c + 64, :] = hot(tt[...] == iota((64, T), 0) + c)
    for c in range(0, 3 * V, 64):
        at = iota((64, T), 0) + c
        total = jnp.where(tv[0:1, :] == at, 1.0, 0.0)
        total = total + jnp.where(tv[1:2, :] == at, 1.0, 0.0)
        total = total + jnp.where(tv[2:3, :] == at, 1.0, 0.0)
        ct[c : c + 64, :] = total.astype(BF16)

    def flag(cond):
        return jnp.where(cond, 1.0, 0.0).astype(F32)

    has_before, has_after = flag(me > 0), flag(me < N - 1)
    build_matrix(mc, mv, m, has_before, has_after, bh, bl)

    def apply(x, hi_ref, lo_ref, start=0):
        parts = rows3(x)
        size = x.shape[1]
        out = nn(parts, hi_ref[start : start + size, :]) + nn(parts, lo_ref[start : start + size, :])
        return add_rows(out)

    for copy in small:
        copy.wait_recv()
    arrived = jnp.concatenate([rx1[0, :, 0:B], rx1[1, :, 0:B]], axis=1)
    c0 = loc[0:1, :] + add_rows(nt(rows3(arrived), rt[...]))
    calcium = add_rows(nn(rows3(c0), gt[...]))
    share = 4.0 * ta[...] * calcium / (calcium + 2.0) / 3.0
    given = add_rows(nt(rows3(share), ct[...]))
    around = jnp.concatenate([rx1[0, :, B:], v[...], rx1[1, :, B:]], axis=1)
    start = m[...] * v[...] - apply(around, bh, bl) * (1.0 / SCALE)
    pk2[:, 0:V] = start + given[:, V : 2 * V]
    pk2[:, V : 2 * V] = given[:, 0:V]
    pk2[:, 2 * V :] = given[:, 2 * V :]

    parts2 = [send(pk2, rx2.at[i], 7 + i, chain(-o)) for i, o in enumerate((-2, -1, 1, 2, 3))]

    for copy in params:
        copy.wait_recv()
    build_matrix(nc, nv, nm, 1.0, flag(me < N - 2), nh, nl)
    for copy in parts2:
        copy.wait_recv()
    own_e, own_b, own_a = pk2[:, 0:V], pk2[:, V : 2 * V], pk2[:, 2 * V :]
    r_own = own_e + rx2[1, :, 2 * V :] + rx2[2, :, V : 2 * V]
    r_before = rx2[1, :, 0:V] + own_b + rx2[0, :, 2 * V :]
    r_after = rx2[2, :, 0:V] + own_a + rx2[3, :, V : 2 * V]
    r_after2 = rx2[3, :, 0:V] + rx2[2, :, 2 * V :] + rx2[4, :, V : 2 * V]
    u_own = apply(jnp.concatenate([r_before, r_own, r_after], axis=1), bh, bl)
    u_after = apply(jnp.concatenate([r_own, r_after, r_after2], axis=1), nh, nl)
    t_own = apply(jnp.concatenate([u_own, 2.0 * u_after], axis=1), bh, bl, V)

    def fold(x):
        return x[:, 0:128] + x[:, 128:256]

    products = (fold(r_own * r_own), fold(r_own * u_own), fold(u_own * u_own), fold(u_own * t_own))
    at = iota((8, 128), 0)
    stack = jnp.zeros((8, 128), F32)
    for i, p in enumerate(products):
        stack = jnp.where(at == i, p, stack)
    sums = jnp.sum(stack, axis=1, keepdims=True)
    red[0] = add_rows(jnp.where(at == iota((8, 128), 1), sums, 0.0))

    def reduce(stage, partner, size, buffer, sem):
        def go(j, carry):
            pltpu.make_async_remote_copy(
                src_ref=red.at[stage], dst_ref=buffer.at[j - 1], send_sem=send_sem.at[sem],
                recv_sem=recv_sem.at[sem], device_id=(partner(j),), device_id_type=MESH,
            ).start()
            return carry

        lax.fori_loop(1, size, go, 0, unroll=True)

    reduce(0, z_partner, ZG, red_a, 12)

    for copy in bulk:
        copy.wait_recv()
    for side in range(2):
        hi, lo = cut2(slots_in[side])
        arr[0:S, side * B : (side + 1) * B] = hi
        arr[S:, side * B : (side + 1) * B] = lo
    for w in range(0, T, 256):
        out = nt(arr[...], rt[w : w + 256, :])
        cnew[:, w : w + 256] = loc[:, w : w + 256] + out[:S, :] + out[S:, :]
    out_copy = pltpu.make_async_copy(cnew, out_h, out_sem.at[0])
    out_copy.start()

    pltpu.make_async_copy(red_a, red_a, recv_sem.at[12]).wait()
    red[1] = red[0] + jnp.sum(red_a[...], axis=0)
    reduce(1, xy_partner, XY, red_b, 13)
    pltpu.make_async_copy(red_b, red_b, recv_sem.at[13]).wait()
    final = red[1] + jnp.sum(red_b[...], axis=0)
    rr, ru, uu, ut = (final[:, i : i + 1] for i in range(4))
    alpha0 = rr / ru
    norm1 = alpha0 * alpha0 * uu - rr
    keep = 1.0 + norm1 / rr
    curve = keep * keep * ru - 2.0 * keep * alpha0 * uu + alpha0 * alpha0 * ut
    alpha1 = norm1 / curve
    direction = keep * r_own - alpha0 * u_own
    vnew[...] = v[...] + (alpha0 * SCALE) * r_own + (alpha1 * SCALE) * direction
    v_copy = pltpu.make_async_copy(vnew, vout_h, out_sem.at[1])
    v_copy.start()
    for copy in sends:
        copy.wait_send()
    pltpu.make_async_copy(red_a, red_a, send_sem.at[12]).wait()
    pltpu.make_async_copy(red_b, red_b, send_sem.at[13]).wait()
    out_copy.wait()
    v_copy.wait()


def per_device(*args):
    shaped = [a.reshape(1, -1) if a.ndim == 1 else a for a in args]
    any_spec = pl.BlockSpec(memory_space=pl.ANY)
    scratch = [pltpu.VMEM(a.shape, a.dtype) for a in shaped]
    scratch += [
        pltpu.VMEM((256, T), BF16),
        pltpu.VMEM((2 * R, T), BF16),
        pltpu.VMEM((2 * S, 4 * T), BF16),
        pltpu.VMEM((T + 2 * B, 4 * T), BF16),
        pltpu.VMEM((S, T), F32),
        pltpu.VMEM((T, 2 * B), BF16),
        pltpu.VMEM((T, T), BF16),
        pltpu.VMEM((3 * V, T), BF16),
        pltpu.VMEM((3 * V, V), BF16),
        pltpu.VMEM((3 * V, V), BF16),
        pltpu.VMEM((3 * V, V), BF16),
        pltpu.VMEM((3 * V, V), BF16),
        pltpu.VMEM((2 * S, 2 * B), BF16),
        pltpu.VMEM((S, T), F32),
        pltpu.VMEM((1, V), F32),
        pltpu.VMEM((2, S, B), F32),
        pltpu.VMEM((2, S, B), F32),
        pltpu.VMEM((2, 1, B + V), F32),
        pltpu.VMEM((2, 1, B + V), F32),
        pltpu.VMEM((8, V), I32),
        pltpu.VMEM((8, V), F32),
        pltpu.VMEM((1, V), F32),
        pltpu.VMEM((1, 3 * V), F32),
        pltpu.VMEM((5, 1, 3 * V), F32),
        pltpu.VMEM((2, 1, 128), F32),
        pltpu.VMEM((ZG - 1, 1, 128), F32),
        pltpu.VMEM((XY - 1, 1, 128), F32),
        pltpu.SemaphoreType.DMA((17,)),
        pltpu.SemaphoreType.DMA((2,)),
        pltpu.SemaphoreType.DMA((14,)),
        pltpu.SemaphoreType.DMA((14,)),
    ]
    counts_new, voltage = pl.pallas_call(
        kernel,
        name="step",
        out_shape=(jax.ShapeDtypeStruct((S, T), F32), jax.ShapeDtypeStruct((1, V), F32)),
        in_specs=[any_spec] * len(shaped),
        out_specs=(any_spec, any_spec),
        scratch_shapes=scratch,
        compiler_params=pltpu.CompilerParams(
            collective_id=1, has_side_effects=True, vmem_limit_bytes=60 * 1024 * 1024
        ),
    )(*shaped)
    return counts_new, voltage.reshape(-1)


def solution(mesh):
    placed = (
        P(None, "dom"), P(), P(), P(), P(None, "dom"), P(), P(None, "dom"), P(None, "dom"), P(None, "dom"),
        P(None, None, "dom"), P("dom"), P(None, "dom"), P("dom"), P("dom"), P("dom"), P(None, "dom"),
        P(None, "dom"),
    )
    return jax.shard_map(
        per_device, mesh=mesh, in_specs=placed, out_specs=(P(None, "dom"), P("dom")), check_vma=False
    )
```

time: 414 us -> 39.4 us (0.10)
  blocking collectives: 325 us -> 0 us
  Pallas kernels: 0 us -> 36.4 us
  local copies, waits for them, and re-layouts: 34 us -> 2.14 us
  starting transfers between devices: 30 us -> 0 us
  waiting for transfers between devices: 8.39 us -> 0 us
  matrix products: 6.46 us -> 0 us
  between operations: 5.17 us -> 0.65 us
    psum x3 -> x0, blocking collectives: 325 us -> none  [the longest x2 221 us: squares_sum(): return lax.psum(jnp.sum(field * field), 'dom')]
    pallas_call x0 -> x1, Pallas kernels: none -> 36.4 us  [per_device(): pl.pallas_call(kernel, name='step', out_shape=(jax.ShapeDtypeStruct((S, T...]
    gather x9 -> x0, local copies, waits for them, and re-layouts: 31.2 us -> none  [the longest x6 25.8 us: apply_matrix(): jnp.take(extended, mat_cols)]
    ppermute x10 -> x0, starting transfers between devices: 30 us -> none  [the longest x5 16.2 us: extended_2(): before = lax.ppermute(last, axis, up)]
    ppermute x10 -> x0, waiting for transfers between devices: 8.39 us -> none  [the longest x5 8.37 us: extended_2(): after = lax.ppermute(initial, axis, down)]
    dot_general x5 -> x0, matrix products: 6.46 us -> none  [the longest x2 3.57 us: add_block(): jnp.dot(amount_piece, onehot, precision=lax.Precision.HIGHEST, preferred_...]
  transfers between devices with their start and end apart: 10 -> 0, of which waited for: 3 -> 0; matrix products, arithmetic and copies ran while one was open for 4% -> 0% of each run, Pallas kernels for 0% -> 0%
where the time goes in v1:
time: 39.4 us; the launch traced here: 39.2 us
  Pallas kernels  36.4 us (92%)
  local copies, waits for them, and re-layouts  2.14 us (5%)
  between operations  0.65 us (2%)
    pallas_call x1, Pallas kernels, per_device(): pl.pallas_call(kernel, name='step', out_shape=(jax.ShapeDtypeStruct((S, T...  36.4 us
    unnamed x4, local copies, waits for them, and re-layouts  2.14 us

profile of v1, /device:TPU:1, one launch (start us, length us, event | category | flops | bytes accessed | tf_op | source)
XLA Modules:
  0.0 39.2 jit_solution(16696548362533397144)
XLA Ops:
  0.6 36.4 %step.1 = (f32[64,512]{1,0:T(8,128)}, f32[1,256]{1,0:T(1,128)}) custom-call(f32[64,512]{1,0:T(8,128)} %counts_h.1, f32[1,256]{1,0:T(1,128)} %bitcast.9, s32[2,256]{1,0:T(2,128)} %ri_h.1, s32[2,256]{1,0:T(2,128)} %pi_h.1, bf16[256,512]{1,0:T(8,128)(2,1)} %leap_h.1, f32[1,64]{1,0:T(1,128)} %bitcast.13, f32[4,512]{1,0:T(4,128)} %fw_h.1, s32[4,512]{1,0:T(4,128)} %ft_h.1, ...), custom_call_target="tpu_custom_call" | custom-call | tf_op jit(solution)/shard_map/step/pallas_call | solution.py:374
  37.1 0.0 copy-start
  37.1 1.6 %copy.21 = f32[64,512]{1,0:T(8,128)} copy(f32[64,512]{1,0:T(8,128)} %get-tuple-element.8) | data formatting | bytes 262144
  38.7 0.0 copy-done
  38.7 0.6 %copy.22 = f32[256]{0:T(256)} copy(f32[256]{0:T(256)S(1)} %bitcast.12) | data formatting | bytes 2048
Async XLA Ops:
  37.1 1.6 %copy-start = (f32[1,256]{1,0:T(1,128)S(1)}, f32[1,256]{1,0:T(1,128)}, u32[]{:S(2)}) copy-start(f32[1,256]{1,0:T(1,128)} %get-tuple-element.5) | copy-start | bytes 3076

commit v2 on v1

--- a/solution.py
+++ b/solution.py
@@ -20,6 +20,23 @@
 SCALE = 1.0 / 32.0
 ZG = 32
 XY = 16
+
+
+HOPS = 4
+PIECES = 2
+NEAR_Z = [h for d in range(HOPS, 0, -1) for h in (d, ZG // 2 - d)]
+
+
+def away(j, sizes):
+    total = 0
+    for size in reversed(sizes):
+        total += min(j % size, size - j % size)
+        j //= size
+    return total
+
+
+Z_ORDER = sorted(range(1, ZG), key=lambda j: -away(j // 2, (16,)))
+XY_ORDER = sorted(range(1, XY), key=lambda j: -away(j, (4, 4)))
 
 
 def nn(a, b):
@@ -91,11 +108,11 @@
 
 def kernel(
     counts_h, rate_h, ri_h, pi_h, leap_h, dr_h, fw_h, ft_h, rr_h, dn_h, tt_h, tv_h, ta_h, v_h, m_h, mc_h, mv_h,
-    out_h, vout_h,
+    out_h, vnew,
     counts, rate, ri, pi, leap, dr, fw, ft, rrow, dn, tt, tv, ta, v, m, mc, mv,
-    xs, fire, am, ot, loc, rt, gt, ct, bh, bl, nh, nl, arr, cnew, vnew,
+    xs, fire, am, ot, loc, rt, gt, ct, bh, bl, nh, nl, arr, cnew,
     slots, slots_in, pk1, rx1, nc, nv, nm, pk2, rx2, red, red_a, red_b,
-    in_sem, out_sem, send_sem, recv_sem,
+    in_sem, out_sem, send_sem, recv_sem, relay_sem,
 ):
     me = lax.axis_index("dom")
     hbm = (counts_h, rate_h, ri_h, pi_h, leap_h, dr_h, fw_h, ft_h, rr_h, dn_h, tt_h, tv_h, ta_h, v_h, m_h, mc_h, mv_h)
@@ -118,8 +135,10 @@
         return lax.rem(xy_at + j, XY) * ZG + z_at
 
     barrier = pltpu.get_barrier_semaphore()
-    greet = [chain(o) for o in (1, -1, 2, -2, 3, -3)]
-    greet += [z_partner(j) for j in range(1, ZG)] + [xy_partner(j) for j in range(1, XY)]
+    greet = [z_base + lax.rem(z_at + 2 * h, ZG) for h in NEAR_Z] + [xy_partner(j) for j in XY_ORDER]
+    other_core = 1 - 2 * lax.rem(me, 2)
+    greet += [z_base + lax.rem(z_at + 2 * h, ZG) + other_core for h in NEAR_Z] + [me + other_core]
+    greet += [chain(o) for o in (3, -3, 2, -2, 1, -1)]
     for other in greet:
         pl.semaphore_signal(barrier, inc=1, device_id=(other,), device_id_type=MESH)
 
@@ -171,30 +190,28 @@
 
     for i in (5, 6, 9):
         loads[i].wait()
-    hop = column(dr[...], S)
-    step = 16
-    for c in range(0, S, step):
-        here = cnew[c : c + step, :]
-        raws = []
-        for f in range(4):
-            prob = hop[c : c + step, :] * fw[f : f + 1, :]
-            mean = here * prob
-            spread = jnp.sqrt(mean * (1.0 - prob))
-            raw = jnp.maximum(mean + spread * dn[f, c : c + step, :].astype(F32), 0.0)
-            raws.append(jnp.where(ft[f : f + 1, :] == T + 2 * B, 0.0, raw))
-        total = raws[0] + raws[1] + raws[2] + raws[3]
-        factor = jnp.minimum(1.0, here / jnp.maximum(total, 1.0))
-        for f in range(4):
-            hi, lo = cut2(raws[f] * factor)
-            am[c : c + step, f * T : (f + 1) * T] = hi
-            am[S + c : S + c + step, f * T : (f + 1) * T] = lo
-        loc[c : c + step, :] = here - total * factor
-    for side in range(2):
-        out = nt(am[...], ot[T + side * B : T + (side + 1) * B, :])
-        slots[side] = out[:S, :] + out[S:, :]
+    wall = T + 2 * B
+    here = cnew[0:1, :]
+    prob = dr[0:1, 0:1] * fw[...]
+    mean = here * prob
+    noise = jnp.concatenate([dn[f, 0:1, :].astype(F32) for f in range(4)], axis=0)
+    raw = jnp.maximum(mean + jnp.sqrt(mean * (1.0 - prob)) * noise, 0.0)
+    raw = jnp.where(ft[...] == wall, 0.0, raw)
+    total = add_rows(raw)
+    factor = jnp.minimum(1.0, here / jnp.maximum(total, 1.0))
+    leaves = [rows3(raw[f : f + 1, :] * factor) for f in range(4)]
+
+    def deposit(start, stop):
+        out = nt(leaves[0], ot[start:stop, 0:T])
+        for f in range(1, 4):
+            out = out + nt(leaves[f], ot[start:stop, f * T : (f + 1) * T])
+        return add_rows(out)
+
+    out = deposit(T, T + 2 * B)
+    pk1[0, :, 0:B] = out[:, 0:B]
+    pk1[1, :, 0:B] = out[:, B:]
     loads[13].wait()
     for side in range(2):
-        pk1[side, :, 0:B] = slots[side, 0:1, :]
         pk1[side, :, B:] = v[...]
 
     for i in (14, 15, 16):
@@ -212,13 +229,13 @@
         return copy
 
     before, after = chain(-1), chain(1)
+    for h in (HOPS, ZG // 2 - HOPS):
+        other = z_base + lax.rem(z_at + 2 * h, ZG)
+        pl.semaphore_signal(relay_sem, inc=1, device_id=(other,), device_id_type=MESH)
     small = [send(pk1.at[1], rx1.at[0], 0, after), send(pk1.at[0], rx1.at[1], 1, before)]
     params = [send(mc, nc, 2, before), send(mv, nv, 3, before), send(m, nm, 4, before)]
-    bulk = [send(slots.at[1], slots_in.at[0], 5, after), send(slots.at[0], slots_in.at[1], 6, before)]
-
-    for w in range(0, T, 256):
-        out = nt(am[...], ot[w : w + 256, :])
-        loc[:, w : w + 256] = loc[:, w : w + 256] + out[:S, :] + out[S:, :]
+
+    first_loc = here - total * factor + deposit(0, T)
     loads[8].wait()
     loads[10].wait()
     loads[11].wait()
@@ -250,7 +267,7 @@
     for copy in small:
         copy.wait_recv()
     arrived = jnp.concatenate([rx1[0, :, 0:B], rx1[1, :, 0:B]], axis=1)
-    c0 = loc[0:1, :] + add_rows(nt(rows3(arrived), rt[...]))
+    c0 = first_loc + add_rows(nt(rows3(arrived), rt[...]))
     calcium = add_rows(nn(rows3(c0), gt[...]))
     share = 4.0 * ta[...] * calcium / (calcium + 2.0) / 3.0
     given = add_rows(nt(rows3(share), ct[...]))
@@ -265,6 +282,31 @@
     for copy in params:
         copy.wait_recv()
     build_matrix(nc, nv, nm, 1.0, flag(me < N - 2), nh, nl)
+    hop = column(dr[...], S)
+    step = 16
+    for c in range(0, S, step):
+        here = cnew[c : c + step, :]
+        raws = []
+        for f in range(4):
+            prob = hop[c : c + step, :] * fw[f : f + 1, :]
+            mean = here * prob
+            spread = jnp.sqrt(mean * (1.0 - prob))
+            raw = jnp.maximum(mean + spread * dn[f, c : c + step, :].astype(F32), 0.0)
+            raws.append(jnp.where(ft[f : f + 1, :] == wall, 0.0, raw))
+        total = raws[0] + raws[1] + raws[2] + raws[3]
+        factor = jnp.minimum(1.0, here / jnp.maximum(total, 1.0))
+        for f in range(4):
+            hi, lo = cut2(raws[f] * factor)
+            am[c : c + step, f * T : (f + 1) * T] = hi
+            am[S + c : S + c + step, f * T : (f + 1) * T] = lo
+        loc[c : c + step, :] = here - total * factor
+    for side in range(2):
+        out = nt(am[...], ot[T + side * B : T + (side + 1) * B, :])
+        slots[side] = out[:S, :] + out[S:, :]
+    bulk = [send(slots.at[1], slots_in.at[0], 5, after), send(slots.at[0], slots_in.at[1], 6, before)]
+    for w in range(0, T, 256):
+        out = nt(am[...], ot[w : w + 256, :])
+        loc[:, w : w + 256] = loc[:, w : w + 256] + out[:S, :] + out[S:, :]
     for copy in parts2:
         copy.wait_recv()
     own_e, own_b, own_a = pk2[:, 0:V], pk2[:, V : 2 * V], pk2[:, 2 * V :]
@@ -287,17 +329,15 @@
     sums = jnp.sum(stack, axis=1, keepdims=True)
     red[0] = add_rows(jnp.where(at == iota((8, 128), 1), sums, 0.0))
 
-    def reduce(stage, partner, size, buffer, sem):
-        def go(j, carry):
+    def reduce(stage, partner, order, buffer, sem):
+        for j in order:
             pltpu.make_async_remote_copy(
                 src_ref=red.at[stage], dst_ref=buffer.at[j - 1], send_sem=send_sem.at[sem],
                 recv_sem=recv_sem.at[sem], device_id=(partner(j),), device_id_type=MESH,
             ).start()
-            return carry
-
-        lax.fori_loop(1, size, go, 0, unroll=True)
-
-    reduce(0, z_partner, ZG, red_a, 12)
+
+    pl.semaphore_wait(relay_sem, 2)
+    reduce(0, z_partner, Z_ORDER, red_a, 12)
 
     for copy in bulk:
         copy.wait_recv()
@@ -308,12 +348,13 @@
     for w in range(0, T, 256):
         out = nt(arr[...], rt[w : w + 256, :])
         cnew[:, w : w + 256] = loc[:, w : w + 256] + out[:S, :] + out[S:, :]
-    out_copy = pltpu.make_async_copy(cnew, out_h, out_sem.at[0])
+
+    out_copy = pltpu.make_async_copy(cnew, out_h, out_sem)
     out_copy.start()
 
     pltpu.make_async_copy(red_a, red_a, recv_sem.at[12]).wait()
     red[1] = red[0] + jnp.sum(red_a[...], axis=0)
-    reduce(1, xy_partner, XY, red_b, 13)
+    reduce(1, xy_partner, XY_ORDER, red_b, 13)
     pltpu.make_async_copy(red_b, red_b, recv_sem.at[13]).wait()
     final = red[1] + jnp.sum(red_b[...], axis=0)
     rr, ru, uu, ut = (final[:, i : i + 1] for i in range(4))
@@ -324,14 +365,28 @@
     alpha1 = norm1 / curve
     direction = keep * r_own - alpha0 * u_own
     vnew[...] = v[...] + (alpha0 * SCALE) * r_own + (alpha1 * SCALE) * direction
-    v_copy = pltpu.make_async_copy(vnew, vout_h, out_sem.at[1])
-    v_copy.start()
     for copy in sends:
         copy.wait_send()
     pltpu.make_async_copy(red_a, red_a, send_sem.at[12]).wait()
     pltpu.make_async_copy(red_b, red_b, send_sem.at[13]).wait()
     out_copy.wait()
-    v_copy.wait()
+
+
+def finish(counts_in, v_in, counts_out, v_out, hold, hold_v, in_sem, out_sem):
+    rows = S // PIECES
+    parts = [slice(i * rows, (i + 1) * rows) for i in range(PIECES)]
+    loads = [pltpu.make_async_copy(v_in, hold_v, in_sem.at[PIECES])]
+    stores = [pltpu.make_async_copy(hold_v, v_out, out_sem.at[PIECES])]
+    for i, part in enumerate(parts):
+        loads.append(pltpu.make_async_copy(counts_in.at[part, :], hold.at[part, :], in_sem.at[i]))
+        stores.append(pltpu.make_async_copy(hold.at[part, :], counts_out.at[part, :], out_sem.at[i]))
+    for copy in loads:
+        copy.start()
+    for load, store in zip(loads, stores):
+        load.wait()
+        store.start()
+    for copy in stores:
+        copy.wait()
 
 
 def per_device(*args):
@@ -353,7 +408,6 @@
         pltpu.VMEM((3 * V, V), BF16),
         pltpu.VMEM((2 * S, 2 * B), BF16),
         pltpu.VMEM((S, T), F32),
-        pltpu.VMEM((1, V), F32),
         pltpu.VMEM((2, S, B), F32),
         pltpu.VMEM((2, S, B), F32),
         pltpu.VMEM((2, 1, B + V), F32),
@@ -367,21 +421,36 @@
         pltpu.VMEM((ZG - 1, 1, 128), F32),
         pltpu.VMEM((XY - 1, 1, 128), F32),
         pltpu.SemaphoreType.DMA((17,)),
-        pltpu.SemaphoreType.DMA((2,)),
+        pltpu.SemaphoreType.DMA,
         pltpu.SemaphoreType.DMA((14,)),
         pltpu.SemaphoreType.DMA((14,)),
+        pltpu.SemaphoreType.REGULAR,
     ]
     counts_new, voltage = pl.pallas_call(
         kernel,
         name="step",
         out_shape=(jax.ShapeDtypeStruct((S, T), F32), jax.ShapeDtypeStruct((1, V), F32)),
         in_specs=[any_spec] * len(shaped),
-        out_specs=(any_spec, any_spec),
+        out_specs=(any_spec, pl.BlockSpec(memory_space=pltpu.VMEM)),
         scratch_shapes=scratch,
         compiler_params=pltpu.CompilerParams(
             collective_id=1, has_side_effects=True, vmem_limit_bytes=60 * 1024 * 1024
         ),
     )(*shaped)
+    counts_new, voltage = pl.pallas_call(
+        finish,
+        name="finish",
+        out_shape=(jax.ShapeDtypeStruct((S, T), F32), jax.ShapeDtypeStruct((1, V), F32)),
+        in_specs=[any_spec, any_spec],
+        out_specs=(any_spec, any_spec),
+        scratch_shapes=[
+            pltpu.VMEM((S, T), F32),
+            pltpu.VMEM((1, V), F32),
+            pltpu.SemaphoreType.DMA((PIECES + 1,)),
+            pltpu.SemaphoreType.DMA((PIECES + 1,)),
+        ],
+        compiler_params=pltpu.CompilerParams(vmem_limit_bytes=60 * 1024 * 1024),
+    )(counts_new, voltage)
     return counts_new, voltage.reshape(-1)
 
 

time: 39.4 us -> 37.7 us (0.957)
  local copies, waits for them, and re-layouts: 2.14 us -> 0 us
  Pallas kernels: 36.4 us -> 36.8 us
    unnamed x4 -> x0, local copies, waits for them, and re-layouts: 2.14 us -> none
    pallas_call x0 -> x1, Pallas kernels: none -> 1.56 us  [per_device(): pl.pallas_call(finish, name='finish', out_shape=(jax.ShapeDtypeStruct((S,...]
    pallas_call x1, Pallas kernels: 36.4 us -> 35.3 us  [per_device(): pl.pallas_call(kernel, name='step', out_shape=(jax.ShapeDtypeStruct((S, T...]
where the time goes in v2:
time: 37.7 us; the launch traced here: 37.5 us
  Pallas kernels  36.8 us (98%)
  between operations  0.65 us (2%)
    pallas_call x1, Pallas kernels, per_device(): pl.pallas_call(kernel, name='step', out_shape=(jax.ShapeDtypeStruct((S, T...  35.3 us
    pallas_call x1, Pallas kernels, per_device(): pl.pallas_call(finish, name='finish', out_shape=(jax.ShapeDtypeStruct((S,...  1.56 us

profile of v2, /device:TPU:1, one launch (start us, length us, event | category | flops | bytes accessed | tf_op | source)
XLA Modules:
  0.0 37.5 jit_solution(896760117200251483)
XLA Ops:
  0.6 35.3 %step.1 = (f32[64,512]{1,0:T(8,128)}, f32[1,256]{1,0:T(1,128)}) custom-call(f32[64,512]{1,0:T(8,128)} %counts_h.1, f32[1,256]{1,0:T(1,128)} %bitcast.9, s32[2,256]{1,0:T(2,128)} %ri_h.1, s32[2,256]{1,0:T(2,128)} %pi_h.1, bf16[256,512]{1,0:T(8,128)(2,1)} %leap_h.1, f32[1,64]{1,0:T(1,128)} %bitcast.12, f32[4,512]{1,0:T(4,128)} %fw_h.1, s32[4,512]{1,0:T(4,128)} %ft_h.1, ...), custom_call_target="tpu_custom_call" | custom-call | tf_op jit(solution)/shard_map/step/pallas_call | solution.py:429
  35.9 1.6 %finish.1 = (f32[64,512]{1,0:T(8,128)}, f32[1,256]{1,0:T(1,128)}) custom-call(f32[64,512]{1,0:T(8,128)} %get-tuple-element.6.counts_in, f32[1,256]{1,0:T(1,128)} %get-tuple-element.7.v_in), custom_call_target="tpu_custom_call" | custom-call | tf_op jit(solution)/shard_map/finish/pallas_call | solution.py:440

commit v3 on v2

--- a/solution.py
+++ b/solution.py
@@ -22,7 +22,8 @@
 XY = 16
 
 
-HOPS = 4
+HOPS = 2
+XY_SIDE = 4
 PIECES = 2
 NEAR_Z = [h for d in range(HOPS, 0, -1) for h in (d, ZG // 2 - d)]
 
@@ -36,7 +37,9 @@
 
 
 Z_ORDER = sorted(range(1, ZG), key=lambda j: -away(j // 2, (16,)))
-XY_ORDER = sorted(range(1, XY), key=lambda j: -away(j, (4, 4)))
+XY_ORDER = sorted(range(1, XY), key=lambda j: -away(j, (XY_SIDE, XY_SIDE)))
+NEAR_XY = [j for j in XY_ORDER if away(j, (XY_SIDE, XY_SIDE)) <= HOPS]
+XY_MIDDLE = (2 * XY_SIDE, 2)
 
 
 def nn(a, b):
@@ -76,10 +79,35 @@
     return jnp.sum(x, axis=0, keepdims=True)
 
 
-def column(row, size):
-    return jnp.sum(
-        jnp.where(iota((size, size), 0) == iota((size, size), 1), row, 0.0), axis=1, keepdims=True
-    )
+def column(row):
+    size = min(row.shape[1], 128)
+    same = iota((size, size), 0) == iota((size, size), 1)
+    blocks = [
+        jnp.sum(jnp.where(same, row[:, at : at + size], 0.0), axis=1, keepdims=True)
+        for at in range(0, row.shape[1], size)
+    ]
+    return blocks[0] if len(blocks) == 1 else jnp.concatenate(blocks, axis=0)
+
+
+def split3(x):
+    hi = x.astype(BF16).astype(F32)
+    rest = x - hi
+    mid = rest.astype(BF16).astype(F32)
+    return hi, mid, rest - mid
+
+
+def by_block(x, index):
+    at = (index >> 7) == iota((8, x.shape[1]), 0)
+    parts = [jnp.where(at, part, 0.0) for part in split3(x)]
+    return jnp.concatenate(parts + [jnp.zeros((8, x.shape[1]), F32)], axis=0).astype(BF16)
+
+
+def low_hot(index):
+    return hot((index & 127) == iota((128, index.shape[1]), 0))
+
+
+def groups(x):
+    return x[0:8, :] + x[8:16, :] + x[16:24, :]
 
 
 def hot(cond):
@@ -110,7 +138,7 @@
     counts_h, rate_h, ri_h, pi_h, leap_h, dr_h, fw_h, ft_h, rr_h, dn_h, tt_h, tv_h, ta_h, v_h, m_h, mc_h, mv_h,
     out_h, vnew,
     counts, rate, ri, pi, leap, dr, fw, ft, rrow, dn, tt, tv, ta, v, m, mc, mv,
-    xs, fire, am, ot, loc, rt, gt, ct, bh, bl, nh, nl, arr, cnew,
+    xs, sel, fire, am, ot, loc, rt, fb, rb, tb, vb, bh, bl, nh, nl, arr, cnew,
     slots, slots_in, pk1, rx1, nc, nv, nm, pk2, rx2, red, red_a, red_b,
     in_sem, out_sem, send_sem, recv_sem, relay_sem,
 ):
@@ -132,45 +160,51 @@
         return z_base + lax.rem(z_at + j, ZG)
 
     def xy_partner(j):
-        return lax.rem(xy_at + j, XY) * ZG + z_at
+        x = lax.rem(xy_at // XY_SIDE + j // XY_SIDE, XY_SIDE)
+        y = lax.rem(lax.rem(xy_at, XY_SIDE) + j % XY_SIDE, XY_SIDE)
+        return (x * XY_SIDE + y) * ZG + z_at
+
+    def z_chip(h):
+        return z_base + lax.rem(z_at + 2 * h, ZG)
 
     barrier = pltpu.get_barrier_semaphore()
-    greet = [z_base + lax.rem(z_at + 2 * h, ZG) for h in NEAR_Z] + [xy_partner(j) for j in XY_ORDER]
     other_core = 1 - 2 * lax.rem(me, 2)
-    greet += [z_base + lax.rem(z_at + 2 * h, ZG) + other_core for h in NEAR_Z] + [me + other_core]
-    greet += [chain(o) for o in (3, -3, 2, -2, 1, -1)]
+    greet = [chain(o) for o in (3, -3, 2, -2, 1, -1)] + [xy_partner(j) for j in NEAR_XY]
+    greet += [z_chip(h) for h in NEAR_Z] + [z_chip(h) + other_core for h in NEAR_Z] + [me + other_core]
     for other in greet:
         pl.semaphore_signal(barrier, inc=1, device_id=(other,), device_id_type=MESH)
 
     loads[7].wait()
 
-    def build_targets(c, carry):
-        at = iota((64, T), 0) + c * 64
-        start = pl.multiple_of(c * 64, 64)
-        for f in range(4):
-            ot[pl.ds(start, 64), f * T : (f + 1) * T] = hot(ft[f : f + 1, :] == at)
-        return carry
-
-    lax.fori_loop(0, (T + 2 * B) // 64, build_targets, 0)
-
-    for i in (0, 1, 2, 3, 4):
+    for f in range(4):
+        fb[:, f * T : (f + 1) * T] = low_hot(ft[f : f + 1, :])
+
+    for i in (1, 2, 3):
         loads[i].wait()
+    lane = iota((1, 256), 1)
+    wanted = jnp.where(lane < 3 * S, lax.rem(lane, S), jnp.where(lane == 3 * S, S, -1)).astype(F32)
+    first = column(ri[0:1, :].astype(F32))
+    second = column(ri[1:2, :].astype(F32))
+    rates = column(rate[...])
+    sel[:, 0:256] = hot(first == wanted)
+    sel[:, 256:] = hot(second == wanted)
+    cap_first = jnp.where(first == S, BIG, 0.0)
+    cap_second = jnp.where(second == S, BIG, 0.0)
+    level = iota((S, R), 0)
+
+    def has(row):
+        return jnp.where(row == level, 1.0, 0.0)
+
+    stoich = (has(pi[0:1, :]) + has(pi[1:2, :]) - has(ri[0:1, :]) - has(ri[1:2, :])).astype(BF16)
+    loads[0].wait()
     for i, part in enumerate(cut3(counts[...])):
         xs[i * S : (i + 1) * S, :] = part
     xs[3 * S :, :] = jnp.ones((S, T), BF16)
-    lane = iota((1, 256), 1)
-    wanted = jnp.where(lane < 3 * S, lax.rem(lane, S), jnp.where(lane == 3 * S, S, -1)).astype(F32)
-    first = column(ri[0:1, :].astype(F32), R)
-    second = column(ri[1:2, :].astype(F32), R)
-    rates = column(rate[...], R)
-    cap_first = jnp.where(first == S, BIG, 0.0)
-    cap_second = jnp.where(second == S, BIG, 0.0)
+    loads[4].wait()
     step = 64
     for c in range(0, R, step):
-        one = first[c : c + step, :]
-        two = second[c : c + step, :]
-        x1 = nn(hot(one == wanted), xs[...])
-        x2 = nn(hot(two == wanted), xs[...])
+        x1 = nn(sel[c : c + step, 0:256], xs[...])
+        x2 = nn(sel[c : c + step, 256:], xs[...])
         prop = rates[c : c + step, :] * x1 * x2
         limit = jnp.minimum(
             jnp.maximum(x1, cap_first[c : c + step, :]), jnp.maximum(x2, cap_second[c : c + step, :])
@@ -179,12 +213,6 @@
         hi, lo = cut2(jnp.minimum(jnp.maximum(raw, 0.0), limit))
         fire[c : c + step, :] = hi
         fire[R + c : R + c + step, :] = lo
-    level = iota((S, R), 0)
-
-    def has(row):
-        return jnp.where(row == level, 1.0, 0.0)
-
-    stoich = (has(pi[0:1, :]) + has(pi[1:2, :]) - has(ri[0:1, :]) - has(ri[1:2, :])).astype(BF16)
     delta = nn(stoich, fire[0:R, :]) + nn(stoich, fire[R:, :])
     cnew[...] = jnp.maximum(counts[...] + delta, 0.0)
 
@@ -199,17 +227,14 @@
     raw = jnp.where(ft[...] == wall, 0.0, raw)
     total = add_rows(raw)
     factor = jnp.minimum(1.0, here / jnp.maximum(total, 1.0))
-    leaves = [rows3(raw[f : f + 1, :] * factor) for f in range(4)]
-
-    def deposit(start, stop):
-        out = nt(leaves[0], ot[start:stop, 0:T])
-        for f in range(1, 4):
-            out = out + nt(leaves[f], ot[start:stop, f * T : (f + 1) * T])
-        return add_rows(out)
-
-    out = deposit(T, T + 2 * B)
-    pk1[0, :, 0:B] = out[:, 0:B]
-    pk1[1, :, 0:B] = out[:, B:]
+    stays = here - total * factor
+    leaves = [by_block(raw[f : f + 1, :] * factor, ft[f : f + 1, :]) for f in range(4)]
+    out = groups(nt(jnp.concatenate(leaves, axis=1), fb[...]))
+    own = out + jnp.concatenate([stays[:, a * 128 : (a + 1) * 128] for a in range(4)] * 2, axis=0)
+    for side in range(2):
+        for a in range(2):
+            row = T // 128 + 2 * side + a
+            pk1[side, :, a * 128 : (a + 1) * 128] = out[row : row + 1, :]
     loads[13].wait()
     for side in range(2):
         pk1[side, :, B:] = v[...]
@@ -229,34 +254,37 @@
         return copy
 
     before, after = chain(-1), chain(1)
-    for h in (HOPS, ZG // 2 - HOPS):
-        other = z_base + lax.rem(z_at + 2 * h, ZG)
-        pl.semaphore_signal(relay_sem, inc=1, device_id=(other,), device_id_type=MESH)
+    def relay(others, level):
+        for other in others:
+            pl.semaphore_signal(relay_sem.at[level], inc=1, device_id=(other,), device_id_type=MESH)
+
     small = [send(pk1.at[1], rx1.at[0], 0, after), send(pk1.at[0], rx1.at[1], 1, before)]
+    relay([z_chip(HOPS), z_chip(ZG // 2 - HOPS)], 0)
+    relay([xy_partner(j) for j in XY_MIDDLE], 1)
     params = [send(mc, nc, 2, before), send(mv, nv, 3, before), send(m, nm, 4, before)]
 
-    first_loc = here - total * factor + deposit(0, T)
-    loads[8].wait()
-    loads[10].wait()
-    loads[11].wait()
-    loads[12].wait()
-    for c in range(0, T, 64):
-        at = iota((64, B), 0) + c
-        rt[c : c + 64, 0:B] = hot(rrow[0:1, :] == at)
-        rt[c : c + 64, B:] = hot(rrow[1:2, :] == at)
-        gt[c : c + 64, :] = hot(tt[...] == iota((64, T), 0) + c)
-    for c in range(0, 3 * V, 64):
-        at = iota((64, T), 0) + c
-        total = jnp.where(tv[0:1, :] == at, 1.0, 0.0)
-        total = total + jnp.where(tv[1:2, :] == at, 1.0, 0.0)
-        total = total + jnp.where(tv[2:3, :] == at, 1.0, 0.0)
-        ct[c : c + 64, :] = total.astype(BF16)
+    for i in (8, 10, 11, 12):
+        loads[i].wait()
+    recv = jnp.concatenate([rrow[0:1, :], rrow[1:2, :]], axis=1)
+    rb[...] = low_hot(recv)
+    tb[...] = low_hot(tt[...])
+    for c in range(3):
+        vb[:, c * T : (c + 1) * T] = low_hot(tv[c : c + 1, :])
 
     def flag(cond):
         return jnp.where(cond, 1.0, 0.0).astype(F32)
 
     has_before, has_after = flag(me > 0), flag(me < N - 1)
     build_matrix(mc, mv, m, has_before, has_after, bh, bl)
+
+    def build_targets(c, carry):
+        at = iota((64, T), 0) + c * 64
+        start = pl.multiple_of(c * 64, 64)
+        for f in range(4):
+            ot[pl.ds(start, 64), f * T : (f + 1) * T] = hot(ft[f : f + 1, :] == at)
+        return carry
+
+    lax.fori_loop(0, (T + 2 * B) // 64, build_targets, 0)
 
     def apply(x, hi_ref, lo_ref, start=0):
         parts = rows3(x)
@@ -267,22 +295,62 @@
     for copy in small:
         copy.wait_recv()
     arrived = jnp.concatenate([rx1[0, :, 0:B], rx1[1, :, 0:B]], axis=1)
-    c0 = first_loc + add_rows(nt(rows3(arrived), rt[...]))
-    calcium = add_rows(nn(rows3(c0), gt[...]))
+    c0 = own + groups(nt(by_block(arrived, recv), rb[...]))
+    parts = jnp.concatenate(split3(c0) + (jnp.zeros((8, 128), F32),), axis=0).astype(BF16)
+    picked = groups(nn(parts, tb[...]))
+    calcium = add_rows(jnp.where((tt[...] >> 7) == iota((8, T), 0), picked, 0.0))
     share = 4.0 * ta[...] * calcium / (calcium + 2.0) / 3.0
-    given = add_rows(nt(rows3(share), ct[...]))
+    corners = jnp.concatenate([by_block(share, tv[c : c + 1, :]) for c in range(3)], axis=1)
+    given = groups(nt(corners, vb[...]))
     around = jnp.concatenate([rx1[0, :, B:], v[...], rx1[1, :, B:]], axis=1)
     start = m[...] * v[...] - apply(around, bh, bl) * (1.0 / SCALE)
-    pk2[:, 0:V] = start + given[:, V : 2 * V]
-    pk2[:, V : 2 * V] = given[:, 0:V]
-    pk2[:, 2 * V :] = given[:, 2 * V :]
+    for a in range(2):
+        half = slice(a * 128, (a + 1) * 128)
+        pk2[:, half] = start[:, half] + given[2 + a : 3 + a, :]
+        pk2[:, V + a * 128 : V + (a + 1) * 128] = given[a : a + 1, :]
+        pk2[:, 2 * V + a * 128 : 2 * V + (a + 1) * 128] = given[4 + a : 5 + a, :]
 
     parts2 = [send(pk2, rx2.at[i], 7 + i, chain(-o)) for i, o in enumerate((-2, -1, 1, 2, 3))]
 
+    pl.semaphore_wait(relay_sem.at[0], 2)
+    relay([z_chip(2 * HOPS), z_chip(ZG // 2 - 2 * HOPS)], 2)
     for copy in params:
         copy.wait_recv()
     build_matrix(nc, nv, nm, 1.0, flag(me < N - 2), nh, nl)
-    hop = column(dr[...], S)
+    for copy in parts2:
+        copy.wait_recv()
+    own_e, own_b, own_a = pk2[:, 0:V], pk2[:, V : 2 * V], pk2[:, 2 * V :]
+    r_own = own_e + rx2[1, :, 2 * V :] + rx2[2, :, V : 2 * V]
+    r_before = rx2[1, :, 0:V] + own_b + rx2[0, :, 2 * V :]
+    r_after = rx2[2, :, 0:V] + own_a + rx2[3, :, V : 2 * V]
+    r_after2 = rx2[3, :, 0:V] + rx2[2, :, 2 * V :] + rx2[4, :, V : 2 * V]
+    u_own = apply(jnp.concatenate([r_before, r_own, r_after], axis=1), bh, bl)
+    u_after = apply(jnp.concatenate([r_own, r_after, r_after2], axis=1), nh, nl)
+    t_own = apply(jnp.concatenate([u_own, 2.0 * u_after], axis=1), bh, bl, V)
+
+    def fold(x):
+        return x[:, 0:128] + x[:, 128:256]
+
+    products = (fold(r_own * r_own), fold(r_own * u_own), fold(u_own * u_own), fold(u_own * t_own))
+    at = iota((8, 128), 0)
+    stack = jnp.zeros((8, 128), F32)
+    for i, p in enumerate(products):
+        stack = jnp.where(at == i, p, stack)
+    sums = jnp.sum(stack, axis=1, keepdims=True)
+    red[0] = add_rows(jnp.where(at == iota((8, 128), 1), sums, 0.0))
+
+    def reduce(stage, partner, order, buffer, sem):
+        for j in order:
+            pltpu.make_async_remote_copy(
+                src_ref=red.at[stage], dst_ref=buffer.at[j - 1], send_sem=send_sem.at[sem],
+                recv_sem=recv_sem.at[sem], device_id=(partner(j),), device_id_type=MESH,
+            ).start()
+
+    pl.semaphore_wait(relay_sem.at[2], 2)
+    reduce(0, z_partner, Z_ORDER, red_a, 12)
+
+
+    hop = column(dr[...])
     step = 16
     for c in range(0, S, step):
         here = cnew[c : c + step, :]
@@ -301,43 +369,21 @@
             am[S + c : S + c + step, f * T : (f + 1) * T] = lo
         loc[c : c + step, :] = here - total * factor
     for side in range(2):
-        out = nt(am[...], ot[T + side * B : T + (side + 1) * B, :])
+        out = nt(ot[T + side * B : T + (side + 1) * B, :], am[...]).T
         slots[side] = out[:S, :] + out[S:, :]
     bulk = [send(slots.at[1], slots_in.at[0], 5, after), send(slots.at[0], slots_in.at[1], 6, before)]
     for w in range(0, T, 256):
-        out = nt(am[...], ot[w : w + 256, :])
+        out = nt(ot[w : w + 256, :], am[...]).T
         loc[:, w : w + 256] = loc[:, w : w + 256] + out[:S, :] + out[S:, :]
-    for copy in parts2:
-        copy.wait_recv()
-    own_e, own_b, own_a = pk2[:, 0:V], pk2[:, V : 2 * V], pk2[:, 2 * V :]
-    r_own = own_e + rx2[1, :, 2 * V :] + rx2[2, :, V : 2 * V]
-    r_before = rx2[1, :, 0:V] + own_b + rx2[0, :, 2 * V :]
-    r_after = rx2[2, :, 0:V] + own_a + rx2[3, :, V : 2 * V]
-    r_after2 = rx2[3, :, 0:V] + rx2[2, :, 2 * V :] + rx2[4, :, V : 2 * V]
-    u_own = apply(jnp.concatenate([r_before, r_own, r_after], axis=1), bh, bl)
-    u_after = apply(jnp.concatenate([r_own, r_after, r_after2], axis=1), nh, nl)
-    t_own = apply(jnp.concatenate([u_own, 2.0 * u_after], axis=1), bh, bl, V)
-
-    def fold(x):
-        return x[:, 0:128] + x[:, 128:256]
-
-    products = (fold(r_own * r_own), fold(r_own * u_own), fold(u_own * u_own), fold(u_own * t_own))
-    at = iota((8, 128), 0)
-    stack = jnp.zeros((8, 128), F32)
-    for i, p in enumerate(products):
-        stack = jnp.where(at == i, p, stack)
-    sums = jnp.sum(stack, axis=1, keepdims=True)
-    red[0] = add_rows(jnp.where(at == iota((8, 128), 1), sums, 0.0))
-
-    def reduce(stage, partner, order, buffer, sem):
-        for j in order:
-            pltpu.make_async_remote_copy(
-                src_ref=red.at[stage], dst_ref=buffer.at[j - 1], send_sem=send_sem.at[sem],
-                recv_sem=recv_sem.at[sem], device_id=(partner(j),), device_id_type=MESH,
-            ).start()
-
-    pl.semaphore_wait(relay_sem, 2)
-    reduce(0, z_partner, Z_ORDER, red_a, 12)
+    for c in range(0, T, 64):
+        at = iota((64, B), 0) + c
+        rt[c : c + 64, 0:B] = hot(rrow[0:1, :] == at)
+        rt[c : c + 64, B:] = hot(rrow[1:2, :] == at)
+
+    pltpu.make_async_copy(red_a, red_a, recv_sem.at[12]).wait()
+    red[1] = red[0] + jnp.sum(red_a[...], axis=0)
+    pl.semaphore_wait(relay_sem.at[1], 2)
+    reduce(1, xy_partner, XY_ORDER, red_b, 13)
 
     for copy in bulk:
         copy.wait_recv()
@@ -346,15 +392,12 @@
         arr[0:S, side * B : (side + 1) * B] = hi
         arr[S:, side * B : (side + 1) * B] = lo
     for w in range(0, T, 256):
-        out = nt(arr[...], rt[w : w + 256, :])
+        out = nt(rt[w : w + 256, :], arr[...]).T
         cnew[:, w : w + 256] = loc[:, w : w + 256] + out[:S, :] + out[S:, :]
 
     out_copy = pltpu.make_async_copy(cnew, out_h, out_sem)
     out_copy.start()
 
-    pltpu.make_async_copy(red_a, red_a, recv_sem.at[12]).wait()
-    red[1] = red[0] + jnp.sum(red_a[...], axis=0)
-    reduce(1, xy_partner, XY_ORDER, red_b, 13)
     pltpu.make_async_copy(red_b, red_b, recv_sem.at[13]).wait()
     final = red[1] + jnp.sum(red_b[...], axis=0)
     rr, ru, uu, ut = (final[:, i : i + 1] for i in range(4))
@@ -395,13 +438,16 @@
     scratch = [pltpu.VMEM(a.shape, a.dtype) for a in shaped]
     scratch += [
         pltpu.VMEM((256, T), BF16),
+        pltpu.VMEM((R, 512), BF16),
         pltpu.VMEM((2 * R, T), BF16),
         pltpu.VMEM((2 * S, 4 * T), BF16),
         pltpu.VMEM((T + 2 * B, 4 * T), BF16),
         pltpu.VMEM((S, T), F32),
         pltpu.VMEM((T, 2 * B), BF16),
-        pltpu.VMEM((T, T), BF16),
-        pltpu.VMEM((3 * V, T), BF16),
+        pltpu.VMEM((128, 4 * T), BF16),
+        pltpu.VMEM((128, 2 * B), BF16),
+        pltpu.VMEM((128, T), BF16),
+        pltpu.VMEM((128, 3 * T), BF16),
         pltpu.VMEM((3 * V, V), BF16),
         pltpu.VMEM((3 * V, V), BF16),
         pltpu.VMEM((3 * V, V), BF16),
@@ -424,7 +470,7 @@
         pltpu.SemaphoreType.DMA,
         pltpu.SemaphoreType.DMA((14,)),
         pltpu.SemaphoreType.DMA((14,)),
-        pltpu.SemaphoreType.REGULAR,
+        pltpu.SemaphoreType.REGULAR((3,)),
     ]
     counts_new, voltage = pl.pallas_call(
         kernel,

time: 37.7 us -> 36.1 us (0.958)
  Pallas kernels: 36.8 us -> 35.2 us
    pallas_call x1, Pallas kernels: 35.3 us -> 33.7 us  [per_device(): pl.pallas_call(kernel, name='step', out_shape=(jax.ShapeDtypeStruct((S, T...]
where the time goes in v3:
time: 36.1 us; the launch traced here: 35.9 us
  Pallas kernels  35.2 us (98%)
  between operations  0.65 us (2%)
    pallas_call x1, Pallas kernels, per_device(): pl.pallas_call(kernel, name='step', out_shape=(jax.ShapeDtypeStruct((S, T...  33.7 us
    pallas_call x1, Pallas kernels, per_device(): pl.pallas_call(finish, name='finish', out_shape=(jax.ShapeDtypeStruct((S,...  1.56 us

profile of v3, /device:TPU:1, one launch (start us, length us, event | category | flops | bytes accessed | tf_op | source)
XLA Modules:
  0.0 35.9 jit_solution(3308881890825615113)
XLA Ops:
  0.6 33.7 %step.1 = (f32[64,512]{1,0:T(8,128)}, f32[1,256]{1,0:T(1,128)}) custom-call(f32[64,512]{1,0:T(8,128)} %counts_h.1, f32[1,256]{1,0:T(1,128)} %bitcast.9, s32[2,256]{1,0:T(2,128)} %ri_h.1, s32[2,256]{1,0:T(2,128)} %pi_h.1, bf16[256,512]{1,0:T(8,128)(2,1)} %leap_h.1, f32[1,64]{1,0:T(1,128)} %bitcast.12, f32[4,512]{1,0:T(4,128)} %fw_h.1, s32[4,512]{1,0:T(4,128)} %ft_h.1, ...), custom_call_target="tpu_custom_call" | custom-call | tf_op jit(solution)/shard_map/step/pallas_call | solution.py:475
  34.3 1.6 %finish.1 = (f32[64,512]{1,0:T(8,128)}, f32[1,256]{1,0:T(1,128)}) custom-call(f32[64,512]{1,0:T(8,128)} %get-tuple-element.6.counts_in, f32[1,256]{1,0:T(1,128)} %get-tuple-element.7.v_in), custom_call_target="tpu_custom_call" | custom-call | tf_op jit(solution)/shard_map/finish/pallas_call | solution.py:486

commit v4 on v3

--- a/solution.py
+++ b/solution.py
@@ -196,6 +196,14 @@
         return jnp.where(row == level, 1.0, 0.0)
 
     stoich = (has(pi[0:1, :]) + has(pi[1:2, :]) - has(ri[0:1, :]) - has(ri[1:2, :])).astype(BF16)
+    def build_targets(c, carry):
+        at = iota((64, T), 0) + c * 64
+        start = pl.multiple_of(c * 64, 64)
+        for f in range(4):
+            ot[pl.ds(start, 64), f * T : (f + 1) * T] = hot(ft[f : f + 1, :] == at)
+        return carry
+
+    lax.fori_loop(0, T // 64, build_targets, 0)
     loads[0].wait()
     for i, part in enumerate(cut3(counts[...])):
         xs[i * S : (i + 1) * S, :] = part
@@ -277,14 +285,7 @@
     has_before, has_after = flag(me > 0), flag(me < N - 1)
     build_matrix(mc, mv, m, has_before, has_after, bh, bl)
 
-    def build_targets(c, carry):
-        at = iota((64, T), 0) + c * 64
-        start = pl.multiple_of(c * 64, 64)
-        for f in range(4):
-            ot[pl.ds(start, 64), f * T : (f + 1) * T] = hot(ft[f : f + 1, :] == at)
-        return carry
-
-    lax.fori_loop(0, (T + 2 * B) // 64, build_targets, 0)
+    lax.fori_loop(T // 64, (T + 2 * B) // 64, build_targets, 0)
 
     def apply(x, hi_ref, lo_ref, start=0):
         parts = rows3(x)
@@ -372,6 +373,12 @@
         out = nt(ot[T + side * B : T + (side + 1) * B, :], am[...]).T
         slots[side] = out[:S, :] + out[S:, :]
     bulk = [send(slots.at[1], slots_in.at[0], 5, after), send(slots.at[0], slots_in.at[1], 6, before)]
+
+    pltpu.make_async_copy(red_a, red_a, recv_sem.at[12]).wait()
+    red[1] = red[0] + jnp.sum(red_a[...], axis=0)
+    pl.semaphore_wait(relay_sem.at[1], 2)
+    reduce(1, xy_partner, XY_ORDER, red_b, 13)
+
     for w in range(0, T, 256):
         out = nt(ot[w : w + 256, :], am[...]).T
         loc[:, w : w + 256] = loc[:, w : w + 256] + out[:S, :] + out[S:, :]
@@ -379,11 +386,6 @@
         at = iota((64, B), 0) + c
         rt[c : c + 64, 0:B] = hot(rrow[0:1, :] == at)
         rt[c : c + 64, B:] = hot(rrow[1:2, :] == at)
-
-    pltpu.make_async_copy(red_a, red_a, recv_sem.at[12]).wait()
-    red[1] = red[0] + jnp.sum(red_a[...], axis=0)
-    pl.semaphore_wait(relay_sem.at[1], 2)
-    reduce(1, xy_partner, XY_ORDER, red_b, 13)
 
     for copy in bulk:
         copy.wait_recv()

time: 36.1 us -> 36.4 us (level)
  Pallas kernels: 35.2 us -> 35.6 us
where the time goes in v4:
time: 36.4 us; the launch traced here: 36.2 us
  Pallas kernels  35.6 us (98%)
  between operations  0.65 us (2%)
    pallas_call x1, Pallas kernels, per_device(): pl.pallas_call(kernel, name='step', out_shape=(jax.ShapeDtypeStruct((S, T...  34 us
    pallas_call x1, Pallas kernels, per_device(): pl.pallas_call(finish, name='finish', out_shape=(jax.ShapeDtypeStruct((S,...  1.56 us

profile of v4, /device:TPU:1, one launch (start us, length us, event | category | flops | bytes accessed | tf_op | source)
XLA Modules:
  0.0 36.2 jit_solution(8873852904923467804)
XLA Ops:
  0.6 34.0 %step.1 = (f32[64,512]{1,0:T(8,128)}, f32[1,256]{1,0:T(1,128)}) custom-call(f32[64,512]{1,0:T(8,128)} %counts_h.1, f32[1,256]{1,0:T(1,128)} %bitcast.9, s32[2,256]{1,0:T(2,128)} %ri_h.1, s32[2,256]{1,0:T(2,128)} %pi_h.1, bf16[256,512]{1,0:T(8,128)(2,1)} %leap_h.1, f32[1,64]{1,0:T(1,128)} %bitcast.12, f32[4,512]{1,0:T(4,128)} %fw_h.1, s32[4,512]{1,0:T(4,128)} %ft_h.1, ...), custom_call_target="tpu_custom_call" | custom-call | tf_op jit(solution)/shard_map/step/pallas_call | solution.py:477
  34.7 1.6 %finish.1 = (f32[64,512]{1,0:T(8,128)}, f32[1,256]{1,0:T(1,128)}) custom-call(f32[64,512]{1,0:T(8,128)} %get-tuple-element.6.counts_in, f32[1,256]{1,0:T(1,128)} %get-tuple-element.7.v_in), custom_call_target="tpu_custom_call" | custom-call | tf_op jit(solution)/shard_map/finish/pallas_call | solution.py:488

commit v5 on v4

--- a/solution.py
+++ b/solution.py
@@ -372,13 +372,13 @@
     for side in range(2):
         out = nt(ot[T + side * B : T + (side + 1) * B, :], am[...]).T
         slots[side] = out[:S, :] + out[S:, :]
-    bulk = [send(slots.at[1], slots_in.at[0], 5, after), send(slots.at[0], slots_in.at[1], 6, before)]
 
     pltpu.make_async_copy(red_a, red_a, recv_sem.at[12]).wait()
     red[1] = red[0] + jnp.sum(red_a[...], axis=0)
     pl.semaphore_wait(relay_sem.at[1], 2)
     reduce(1, xy_partner, XY_ORDER, red_b, 13)
 
+    bulk = [send(slots.at[1], slots_in.at[0], 5, after), send(slots.at[0], slots_in.at[1], 6, before)]
     for w in range(0, T, 256):
         out = nt(ot[w : w + 256, :], am[...]).T
         loc[:, w : w + 256] = loc[:, w : w + 256] + out[:S, :] + out[S:, :]

time: 36.4 us -> 37.6 us (1.033)
  Pallas kernels: 35.6 us -> 36.8 us
    pallas_call x1, Pallas kernels: 34 us -> 35.2 us  [per_device(): pl.pallas_call(kernel, name='step', out_shape=(jax.ShapeDtypeStruct((S, T...]
where the time goes in v5:
time: 37.6 us; the launch traced here: 37.4 us
  Pallas kernels  36.8 us (98%)
  between operations  0.65 us (2%)
    pallas_call x1, Pallas kernels, per_device(): pl.pallas_call(kernel, name='step', out_shape=(jax.ShapeDtypeStruct((S, T...  35.2 us
    pallas_call x1, Pallas kernels, per_device(): pl.pallas_call(finish, name='finish', out_shape=(jax.ShapeDtypeStruct((S,...  1.56 us

profile of v5, /device:TPU:1, one launch (start us, length us, event | category | flops | bytes accessed | tf_op | source)
XLA Modules:
  0.0 37.4 jit_solution(6628091671384110210)
XLA Ops:
  0.6 35.2 %step.1 = (f32[64,512]{1,0:T(8,128)}, f32[1,256]{1,0:T(1,128)}) custom-call(f32[64,512]{1,0:T(8,128)} %counts_h.1, f32[1,256]{1,0:T(1,128)} %bitcast.9, s32[2,256]{1,0:T(2,128)} %ri_h.1, s32[2,256]{1,0:T(2,128)} %pi_h.1, bf16[256,512]{1,0:T(8,128)(2,1)} %leap_h.1, f32[1,64]{1,0:T(1,128)} %bitcast.12, f32[4,512]{1,0:T(4,128)} %fw_h.1, s32[4,512]{1,0:T(4,128)} %ft_h.1, ...), custom_call_target="tpu_custom_call" | custom-call | tf_op jit(solution)/shard_map/step/pallas_call | solution.py:477
  35.8 1.6 %finish.1 = (f32[64,512]{1,0:T(8,128)}, f32[1,256]{1,0:T(1,128)}) custom-call(f32[64,512]{1,0:T(8,128)} %get-tuple-element.6.counts_in, f32[1,256]{1,0:T(1,128)} %get-tuple-element.7.v_in), custom_call_target="tpu_custom_call" | custom-call | tf_op jit(solution)/shard_map/finish/pallas_call | solution.py:488

commit v6 on v3

--- a/solution.py
+++ b/solution.py
@@ -24,7 +24,7 @@
 
 HOPS = 2
 XY_SIDE = 4
-PIECES = 2
+PIECES = 1
 NEAR_Z = [h for d in range(HOPS, 0, -1) for h in (d, ZG // 2 - d)]
 
 

time: 36.1 us -> 36.1 us (level)
  no operation moved by 1% of the time
where the time goes in v6:
time: 36.1 us; the launch traced here: 35.9 us
  Pallas kernels  35.3 us (98%)
  between operations  0.65 us (2%)
    pallas_call x1, Pallas kernels, per_device(): pl.pallas_call(kernel, name='step', out_shape=(jax.ShapeDtypeStruct((S, T...  33.7 us
    pallas_call x1, Pallas kernels, per_device(): pl.pallas_call(finish, name='finish', out_shape=(jax.ShapeDtypeStruct((S,...  1.6 us

profile of v6, /device:TPU:1, one launch (start us, length us, event | category | flops | bytes accessed | tf_op | source)
XLA Modules:
  0.0 35.9 jit_solution(15431926703566462803)
XLA Ops:
  0.6 33.7 %step.1 = (f32[64,512]{1,0:T(8,128)}, f32[1,256]{1,0:T(1,128)}) custom-call(f32[64,512]{1,0:T(8,128)} %counts_h.1, f32[1,256]{1,0:T(1,128)} %bitcast.9, s32[2,256]{1,0:T(2,128)} %ri_h.1, s32[2,256]{1,0:T(2,128)} %pi_h.1, bf16[256,512]{1,0:T(8,128)(2,1)} %leap_h.1, f32[1,64]{1,0:T(1,128)} %bitcast.12, f32[4,512]{1,0:T(4,128)} %fw_h.1, s32[4,512]{1,0:T(4,128)} %ft_h.1, ...), custom_call_target="tpu_custom_call" | custom-call | tf_op jit(solution)/shard_map/step/pallas_call | solution.py:475
  34.3 1.6 %finish.1 = (f32[64,512]{1,0:T(8,128)}, f32[1,256]{1,0:T(1,128)}) custom-call(f32[64,512]{1,0:T(8,128)} %get-tuple-element.6.counts_in, f32[1,256]{1,0:T(1,128)} %get-tuple-element.7.v_in), custom_call_target="tpu_custom_call" | custom-call | tf_op jit(solution)/shard_map/finish/pallas_call | solution.py:486
